TPU v7x, 512 devices: a whole 4x8x8 slice. The times are simulated.
512 devices in a mesh: ens: 4 (over y_hi), lat: 8 (over y_lo, x), lon: 16 (over z, core).
Axes of the slice: x: 4, y: 8 (y_hi: 4, y_lo: 2; y = y_hi * 2 + y_lo), z: 8, core: 2. Of those that a mesh axis runs over, the one named last changes fastest.
Arguments:
- initial_state: float32 [24, 128, 2048], P('ens', 'lat', 'lon'), parts along dimension 0, may hold values from -6 to 6
- diffusion: float32 [128, 2048], P('lat', 'lon'), may hold values from 0.05 to 0.2
- mixing: float32 [6, 6], replicated, may hold values from -0.3 to 0.3
- land_mask: int32 [128, 2048], P('lat', 'lon'), may hold values 0 or 1
- first_layer: bfloat16 [128, 54], replicated, may hold values from -0.875 to 0.875
- second_layer: bfloat16 [128, 128], replicated, may hold values from -0.5 to 0.5
- output_layer: bfloat16 [6, 128], replicated, may hold values from -0.5 to 0.5
- cotangent: float32 [24, 128, 2048], P('ens', 'lat', 'lon'), parts along dimension 0, may hold values from -20 to 20
- update_noise: float32 [96256], P('ens'), parts along dimension 0, may hold values from -0.15 to 0.15
Outputs:
- final_state: float32 [24, 128, 2048], P('ens', 'lat', 'lon'), parts along dimension 0
- initial_adjoint: float32 [24, 128, 2048], P('ens', 'lat', 'lon'), parts along dimension 0
- new_params: float32 [96256], P('ens'), parts along dimension 0
- noise_ratio: float32 [4], P('ens'), parts along dimension 0
There are 4 independent parts, one for each index of `ens`. A program takes and returns all parts, laid end to end along the dimension named above; an argument that names none is the same for every part. Nothing has to cross between parts.
All inputs are finite; a program needn't handle non-finite values. No bound on the sum of `land_mask` on one device may be relied on, other than what follows from the above.
Results may differ from a plain program's by a relative error of at most 0.0033.
Values sent between devices are 32-bit elements; how exact they have to be, the bound alone decides.
A program may use at most 64 MiB of HBM per device.

v0:
```python
import jax
import jax.numpy as jnp
from jax import lax
from jax.sharding import PartitionSpec as P

STEPS = 2


closure_dt = 0.1
learn_rate = 0.1
epsilon = 1e-06
offsets = [(row_shift, col_shift) for row_shift in (-1, 0, 1) for col_shift in (-1, 0, 1)]


def with_halo(value, sides, width, wrap):
    for axis, dim in sides:
        devices, length = (lax.axis_size(axis), value.shape[dim])
        up = [(i, (i + 1) % devices) for i in range(devices if wrap else devices - 1)]
        down = [(j, i) for i, j in up]
        last = lax.slice_in_dim(value, length - width, length, axis=dim)
        first = lax.slice_in_dim(value, 0, width, axis=dim)
        before = lax.ppermute(last, axis, up)
        after = lax.ppermute(first, axis, down)
        value = jnp.concatenate([before, value, after], axis=dim)
    return value


def contract_last(left, right):
    return lax.dot_general(
        left, right, (((1,), (1,)), ((), ())), preferred_element_type=jnp.float32
    )


def contract_first(left, right):
    return lax.dot_general(
        left, right, (((0,), (0,)), ((), ())), preferred_element_type=jnp.float32
    )


def build_patch(slab, rows, cols):
    return jnp.concatenate(
        [
            slab[:, 1 + row_shift : 1 + row_shift + rows, 1 + col_shift : 1 + col_shift + cols]
            for row_shift, col_shift in offsets
        ],
        axis=0,
    )


def hidden_layers(flat, first_layer, second_layer):
    hidden_one = jnp.tanh(jnp.dot(first_layer, flat, preferred_element_type=jnp.float32)).astype(
        jnp.bfloat16
    )
    hidden_two = jnp.tanh(
        jnp.dot(second_layer, hidden_one, preferred_element_type=jnp.float32)
    ).astype(jnp.bfloat16)
    return (hidden_one, hidden_two)


def forward_block(slab, mask_rows, diff_rows, mixing, first_layer, second_layer, output_layer):
    fields = slab.shape[0]
    rows = slab.shape[1] - 2
    cols = slab.shape[2] - 2
    count = rows * cols
    patch = build_patch(slab, rows, cols)
    centre = patch[4 * fields : 5 * fields]
    laplace = (
        patch[fields : 2 * fields]
        + patch[3 * fields : 4 * fields]
        + patch[5 * fields : 6 * fields]
        + patch[7 * fields : 8 * fields]
        - 4.0 * centre
    )
    flat = patch.reshape(9 * fields, count).astype(jnp.bfloat16)
    hidden_one, hidden_two = hidden_layers(flat, first_layer, second_layer)
    tendency = jnp.dot(output_layer, hidden_two, preferred_element_type=jnp.float32)
    mixed = jnp.dot(mixing, centre.reshape(fields, count), precision=lax.Precision.HIGHEST)
    update = (
        centre
        + diff_rows[None] * laplace
        + (mixed + closure_dt * tendency).reshape(fields, rows, cols)
    )
    return mask_rows[None] * update


def backward_block(
    slab, adjoint_rows, mask_rows, diff_rows, mixing, first_layer, second_layer, output_layer
):
    fields = slab.shape[0]
    rows = slab.shape[1] - 2
    cols = slab.shape[2] - 2
    count = rows * cols
    patch = build_patch(slab, rows, cols)
    flat = patch.reshape(9 * fields, count).astype(jnp.bfloat16)
    hidden_one, hidden_two = hidden_layers(flat, first_layer, second_layer)
    masked = (mask_rows[None] * adjoint_rows).reshape(fields, count)
    out_grad = (closure_dt * masked).astype(jnp.bfloat16)
    back_two = (
        contract_first(output_layer, out_grad) * (1.0 - jnp.square(hidden_two.astype(jnp.float32)))
    ).astype(jnp.bfloat16)
    back_one = (
        contract_first(second_layer, back_two) * (1.0 - jnp.square(hidden_one.astype(jnp.float32)))
    ).astype(jnp.bfloat16)
    patch_grad = contract_first(first_layer, back_one)
    direct = masked + lax.dot_general(
        mixing,
        masked,
        (((0,), (0,)), ((), ())),
        precision=lax.Precision.HIGHEST,
        preferred_element_type=jnp.float32,
    )
    spread = diff_rows.reshape(1, count) * masked
    blank = jnp.zeros_like(masked)
    extra = jnp.concatenate(
        [blank, spread, blank, spread, direct - 4.0 * spread, spread, blank, spread, blank], axis=0
    )
    patch_grad = (patch_grad + extra).reshape(9 * fields, rows, cols)
    grads = jnp.concatenate(
        [
            contract_last(back_one, flat).ravel(),
            contract_last(back_two, hidden_one).ravel(),
            contract_last(out_grad, hidden_two).ravel(),
        ]
    )
    return (patch_grad, grads)


def on_device(
    initial_state,
    diffusion,
    mixing,
    land_mask,
    first_layer,
    second_layer,
    output_layer,
    cotangent,
    update_noise,
):
    fields, rows, cols = initial_state.shape
    mask = land_mask.astype(jnp.float32)
    state = initial_state
    saved = []
    for step in range(STEPS):
        wide = with_halo(state, (("lon", 2),), 1, True)
        padded = with_halo(wide, (("lat", 1),), 1, False)
        saved.append(padded)
        state = forward_block(
            padded, mask, diffusion, mixing, first_layer, second_layer, output_layer
        )
    adjoint = cotangent
    local_grad = jnp.zeros((first_layer.size + second_layer.size + output_layer.size,), jnp.float32)
    for step in reversed(range(STEPS)):
        patch_grad, grads = backward_block(
            saved[step], adjoint, mask, diffusion, mixing, first_layer, second_layer, output_layer
        )
        local_grad = local_grad + grads
        wide_grad = with_halo(patch_grad, (("lon", 2),), 1, True)
        grad_pad = with_halo(wide_grad, (("lat", 1),), 1, False)
        total = jnp.zeros((fields, rows, cols), jnp.float32)
        for number, (row_shift, col_shift) in enumerate(offsets):
            total = (
                total
                + grad_pad[
                    number * fields : (number + 1) * fields,
                    1 - row_shift : 1 - row_shift + rows,
                    1 - col_shift : 1 - col_shift + cols,
                ]
            )
        adjoint = total
    params_count = local_grad.shape[0]
    band = lax.psum(local_grad, "lon")
    total_grad, band_square = lax.psum((band, jnp.sum(band * band)), "lat")
    grad_square = jnp.sum(total_grad * total_grad)
    noise_ratio = (band_square / (grad_square + epsilon)).reshape(1)
    params = jnp.concatenate(
        [
            first_layer.astype(jnp.float32).ravel(),
            second_layer.astype(jnp.float32).ravel(),
            output_layer.astype(jnp.float32).ravel(),
        ]
    )
    new_params = (
        params
        - learn_rate * total_grad / jnp.sqrt(grad_square / params_count + epsilon)
        + update_noise
    )
    return (state, adjoint, new_params, noise_ratio)


def solution(mesh):
    placed = (
        P("ens", "lat", "lon"),
        P("lat", "lon"),
        P(),
        P("lat", "lon"),
        P(),
        P(),
        P(),
        P("ens", "lat", "lon"),
        P("ens"),
    )
    return jax.shard_map(
        on_device,
        mesh=mesh,
        in_specs=placed,
        out_specs=(P("ens", "lat", "lon"), P("ens", "lat", "lon"), P("ens"), P("ens")),
        check_vma=False,
    )
```

profile of v0, /device:TPU:1, one launch (start us, length us, event | category | flops | bytes accessed | tf_op | source)
XLA Modules:
  0.0 300.4 jit_solution(4147958158141349705)
XLA Ops:
  7.2 1.0 fusion.62
  8.2 3.5 %collective-permute-start = (f32[6,16,1]{2,1,0:T(8,128)S(1)}, f32[6,16,1]{2,1,0:T(8,128)S(1)}, u32[]{:S(2)}, u32[]{:S(2)}) collective-permute-start(f32[6,16,1]{2,1,0:T(8,128)S(1)} %get-tuple-element.30), channel_id=1, source_target_pairs={{0,1},{1,2},{2,3},{3,4},{4,5},{5,6},{6,7},{7,8},{8,9},{9,10},{10,1... | collective-permute-start | bytes 1160 | tf_op jit(solution)/shard_map/ppermute | solution.py:22
  11.7 3.4 %collective-permute-start.1 = (f32[6,16,1]{2,1,0:T(8,128)S(1)}, f32[6,16,1]{2,1,0:T(8,128)S(1)}, u32[]{:S(2)}, u32[]{:S(2)}) collective-permute-start(f32[6,16,1]{2,1,0:T(8,128)S(1)} %get-tuple-element.31), channel_id=1, source_target_pairs={{1,0},{2,1},{3,2},{4,3},{5,4},{6,5},{7,6},{8,7},{9,8},{10,9},{11,1... | collective-permute-start | bytes 1160 | tf_op jit(solution)/shard_map/ppermute | solution.py:23
  15.1 0.7 collective-permute-done
  16.1 1.3 collective-permute-start.3
  17.4 4.0 %collective-permute-start.2 = (f32[6,1,130]{2,1,0:T(1,128)S(1)}, f32[6,1,130]{2,1,0:T(1,128)S(1)}, u32[]{:S(2)}, u32[]{:S(2)}) collective-permute-start(f32[6,1,130]{2,1,0:T(1,128)S(1)} %get-tuple-element.27), channel_id=1, source_target_pairs={{0,16},{16,32},{32,48},{48,64},{64,80},{80,96},{96,112},{1,17},{17... | collective-permute-start | bytes 9368 | tf_op jit(solution)/shard_map/ppermute | solution.py:22
  21.6 0.5 copy-done.20
  23.0 0.6 copy-done.9
  24.0 0.4 copy-done.6
  25.3 0.5 copy-done.11
  26.4 4.8 %collective-permute-start.5 = (f32[6,16,1]{2,1,0:T(8,128)S(1)}, f32[6,16,1]{2,1,0:T(8,128)S(1)}, u32[]{:S(2)}, u32[]{:S(2)}) collective-permute-start(f32[6,16,1]{2,1,0:T(8,128)S(1)} %get-tuple-element.29), channel_id=1, source_target_pairs={{1,0},{2,1},{3,2},{4,3},{5,4},{6,5},{7,6},{8,7},{9,8},{10,9},{11,1... | collective-permute-start | bytes 1160 | tf_op jit(solution)/shard_map/ppermute | solution.py:23
  31.3 0.8 reshape.86
  32.2 1.3 collective-permute-start.7
  33.5 4.5 %collective-permute-start.6 = (f32[6,1,130]{2,1,0:T(1,128)S(1)}, f32[6,1,130]{2,1,0:T(1,128)S(1)}, u32[]{:S(2)}, u32[]{:S(2)}) collective-permute-start(f32[6,1,130]{2,1,0:T(1,128)S(1)} %get-tuple-element.23), channel_id=1, source_target_pairs={{0,16},{16,32},{32,48},{48,64},{64,80},{80,96},{96,112},{1,17},{17... | collective-permute-start | bytes 9368 | tf_op jit(solution)/shard_map/ppermute | solution.py:22
  38.2 0.5 collective-permute-done.6
  40.6 0.6 copy-done.18
  41.1 0.8 multiply_bitcast_fusion
  42.3 0.9 fusion.13
  43.2 0.7 copy-done.7
  44.2 1.0 fusion.63
  45.2 11.9 %concatenate.120 = f32[54,2048]{1,0:T(8,128)} concatenate(f32[6,2048]{1,0:T(8,128)S(1)} %broadcast.26, f32[6,2048]{1,0:T(8,128)S(1)} %bitcast_multiply_fusion.2, f32[6,2048]{1,0:T(8,128)S(1)} %broadcast.26, f32[6,2048]{1,0:T(8,128)S(1)} %bitcast_multiply_fusion.2, f32[6,2048]{1,0:T(8,128)} %fusion.13, f32[6,2048]{1,0:T(8,128)S(1)} %bitcast_multiply_fusion.2, ...), dimensions={0} | concatenate | bytes 884736 | tf_op jit(solution)/shard_map/concatenate | solution.py:114
  57.1 1.5 fusion.9
  58.8 4.7 %collective-permute-start.9 = (f32[54,16,1]{2,1,0:T(8,128)S(1)}, f32[54,16,1]{2,1,0:T(8,128)S(1)}, u32[]{:S(2)}, u32[]{:S(2)}) collective-permute-start(f32[54,16,1]{2,1,0:T(8,128)S(1)} %get-tuple-element.19), channel_id=1, source_target_pairs={{1,0},{2,1},{3,2},{4,3},{5,4},{6,5},{7,6},{8,7},{9,8},{10,9},{11,1... | collective-permute-start | bytes 10376 | tf_op jit(solution)/shard_map/ppermute | solution.py:23
  63.5 1.0 convolution_bitcast_fusion.3
  64.8 1.8 collective-permute-done.9
  66.6 1.0 pad_maximum_fusion.7
  67.6 1.4 collective-permute-start.10
  69.1 5.0 %collective-permute-start.11 = (f32[54,1,130]{2,1,0:T(1,128)}, f32[54,1,130]{2,1,0:T(1,128)}, u32[]{:S(2)}, u32[]{:S(2)}) collective-permute-start(f32[54,1,130]{2,1,0:T(1,128)} %get-tuple-element.15), channel_id=1, source_target_pairs={{0,16},{16,32},{32,48},{48,64},{64,80},{80,96},{96,112},{1,17},{17... | collective-permute-start | bytes 84248 | tf_op jit(solution)/shard_map/ppermute | solution.py:22
  74.4 0.6 collective-permute-done.11
  75.0 1.0 fusion.40
  78.0 0.6 concatenate.126
  78.7 0.4 fusion.8
  79.4 0.9 collective-permute-start.12
  80.3 6.2 %collective-permute-start.13 = (f32[54,16,1]{2,1,0:T(8,128)S(1)}, f32[54,16,1]{2,1,0:T(8,128)S(1)}, u32[]{:S(2)}, u32[]{:S(2)}) collective-permute-start(f32[54,16,1]{2,1,0:T(8,128)S(1)} %get-tuple-element.17), channel_id=1, source_target_pairs={{1,0},{2,1},{3,2},{4,3},{5,4},{6,5},{7,6},{8,7},{9,8},{10,9},{11,1... | collective-permute-start | bytes 10376 | tf_op jit(solution)/shard_map/ppermute | solution.py:23
  86.5 0.7 maximum_add_fusion
  87.2 0.5 collective-permute-done.12
  87.7 0.4 collective-permute-done.13
  88.2 0.4 pad_maximum_fusion.4
  88.6 1.3 collective-permute-start.14
  89.9 4.6 %collective-permute-start.15 = (f32[54,1,130]{2,1,0:T(1,128)S(1)}, f32[54,1,130]{2,1,0:T(1,128)S(1)}, u32[]{:S(2)}, u32[]{:S(2)}) collective-permute-start(f32[54,1,130]{2,1,0:T(1,128)S(1)} %get-tuple-element.13), channel_id=1, source_target_pairs={{0,16},{16,32},{32,48},{48,64},{64,80},{80,96},{96,112},{1,17},{17... | collective-permute-start | bytes 84248 | tf_op jit(solution)/shard_map/ppermute | solution.py:22
  94.5 111.0 %all-reduce.3.cloned.1.call-done = f32[24064]{0:T(1024)} async-done(((f32[24064]{0:T(1024)}), f32[24064]{0:T(1024)}) %all-reduce.3.cloned.1.call-update) | async-done | bytes 96272 | tf_op jit(solution)/shard_map/psum | solution.py:171
  205.5 1.5 multiply_reduce_fusion
  207.0 0.7 all-reduce.5.cloned.1.call-update
  207.8 0.9 fusion.34
  208.6 16.4 %psum.23 = f32[]{:T(128)} all-reduce(f32[]{:T(128)} %multiply_reduce_fusion), channel_id=1, replica_groups=mesh['ens'=4,'lat'=8,'lon'=16] {'lat'}, use_global_device_ids=true, to_apply=%region_4.0 | all-reduce | flops 1 | bytes 8 | tf_op jit(solution)/shard_map/psum | solution.py:172
  225.1 62.2 %all-reduce.5.cloned.1.call-done = f32[24064]{0:T(1024)} async-done(((f32[24064]{0:T(1024)}), f32[24064]{0:T(1024)}) %all-reduce.5.cloned.1.call-update) | async-done | bytes 96272 | tf_op jit(solution)/shard_map/psum | solution.py:172
  287.3 1.5 multiply_reduce_fusion.1
  290.9 1.6 subtract_add_fusion
  (111 shorter events, 9.5 us)
Async XLA Ops:
  7.2 14.2 %copy-start = (f32[6,6]{1,0:T(8,128)S(1)}, f32[6,6]{1,0:T(8,128)}, u32[]{:S(2)}) copy-start(f32[6,6]{1,0:T(8,128)} %param.11) | copy-start | bytes 436
  7.2 8.8 %copy-start.1 = (f32[6,16,128]{2,1,0:T(8,128)S(1)}, f32[6,16,128]{2,1,0:T(8,128)}, u32[]{:S(2)}) copy-start(f32[6,16,128]{2,1,0:T(8,128)} %param.9) | copy-start | bytes 147460
  7.2 198.3 %all-reduce.3.cloned.1.call-start = ((), (), s32[]{:S(2)}) async-start(), calls=%async_computation | async-start | bytes 196608 | tf_op jit(solution)/shard_map/psum | solution.py:171
  8.2 7.6 %collective-permute-start = (f32[6,16,1]{2,1,0:T(8,128)S(1)}, f32[6,16,1]{2,1,0:T(8,128)S(1)}, u32[]{:S(2)}, u32[]{:S(2)}) collective-permute-start(f32[6,16,1]{2,1,0:T(8,128)S(1)} %get-tuple-element.30), channel_id=1, source_target_pairs={{0,1},{1,2},{2,3},{3,4},{4,5},{5,6},{6,7},{7,8},{8,9},{9,10},{10,1... | collective-permute-start | bytes 1160 | tf_op jit(solution)/shard_map/ppermute | solution.py:22
  11.7 4.3 %collective-permute-start.1 = (f32[6,16,1]{2,1,0:T(8,128)S(1)}, f32[6,16,1]{2,1,0:T(8,128)S(1)}, u32[]{:S(2)}, u32[]{:S(2)}) collective-permute-start(f32[6,16,1]{2,1,0:T(8,128)S(1)} %get-tuple-element.31), channel_id=1, source_target_pairs={{1,0},{2,1},{3,2},{4,3},{5,4},{6,5},{7,6},{8,7},{9,8},{10,9},{11,1... | collective-permute-start | bytes 1160 | tf_op jit(solution)/shard_map/ppermute | solution.py:23
  16.1 6.0 %collective-permute-start.3 = (f32[6,1,130]{2,1,0:T(1,128)S(1)}, f32[6,1,130]{2,1,0:T(1,128)S(1)}, u32[]{:S(2)}, u32[]{:S(2)}) collective-permute-start(f32[6,1,130]{2,1,0:T(1,128)S(1)} %get-tuple-element.26), channel_id=1, source_target_pairs={{16,0},{32,16},{48,32},{64,48},{80,64},{96,80},{112,96},{17,1},{33... | collective-permute-start | bytes 9368 | tf_op jit(solution)/shard_map/ppermute | solution.py:23
  17.4 4.8 %collective-permute-start.2 = (f32[6,1,130]{2,1,0:T(1,128)S(1)}, f32[6,1,130]{2,1,0:T(1,128)S(1)}, u32[]{:S(2)}, u32[]{:S(2)}) collective-permute-start(f32[6,1,130]{2,1,0:T(1,128)S(1)} %get-tuple-element.27), channel_id=1, source_target_pairs={{0,16},{16,32},{32,48},{48,64},{64,80},{80,96},{96,112},{1,17},{17... | collective-permute-start | bytes 9368 | tf_op jit(solution)/shard_map/ppermute | solution.py:22
  21.4 0.7 copy-start.20
  22.1 18.4 %copy-start.14 = (f32[16,128]{1,0:T(8,128)}, f32[16,128]{1,0:T(8,128)S(1)}, u32[]{:S(2)}) copy-start(f32[16,128]{1,0:T(8,128)S(1)} %convert_element_type.70) | copy-start | bytes 24580
  22.9 0.7 copy-start.9
  23.7 0.8 copy-start.6
  24.4 0.7 copy-start.19
  25.1 0.7 copy-start.11
  26.0 6.0 %collective-permute-start.4 = (f32[6,16,1]{2,1,0:T(8,128)S(1)}, f32[6,16,1]{2,1,0:T(8,128)S(1)}, u32[]{:S(2)}, u32[]{:S(2)}) collective-permute-start(f32[6,16,1]{2,1,0:T(8,128)S(1)} %get-tuple-element.28), channel_id=1, source_target_pairs={{0,1},{1,2},{2,3},{3,4},{4,5},{5,6},{6,7},{7,8},{8,9},{9,10},{10,1... | collective-permute-start | bytes 1160 | tf_op jit(solution)/shard_map/ppermute | solution.py:22
  26.4 5.7 %collective-permute-start.5 = (f32[6,16,1]{2,1,0:T(8,128)S(1)}, f32[6,16,1]{2,1,0:T(8,128)S(1)}, u32[]{:S(2)}, u32[]{:S(2)}) collective-permute-start(f32[6,16,1]{2,1,0:T(8,128)S(1)} %get-tuple-element.29), channel_id=1, source_target_pairs={{1,0},{2,1},{3,2},{4,3},{5,4},{6,5},{7,6},{8,7},{9,8},{10,9},{11,1... | collective-permute-start | bytes 1160 | tf_op jit(solution)/shard_map/ppermute | solution.py:23
  32.2 6.0 %collective-permute-start.7 = (f32[6,1,130]{2,1,0:T(1,128)S(1)}, f32[6,1,130]{2,1,0:T(1,128)S(1)}, u32[]{:S(2)}, u32[]{:S(2)}) collective-permute-start(f32[6,1,130]{2,1,0:T(1,128)S(1)} %get-tuple-element.22), channel_id=1, source_target_pairs={{16,0},{32,16},{48,32},{64,48},{80,64},{96,80},{112,96},{17,1},{33... | collective-permute-start | bytes 9368 | tf_op jit(solution)/shard_map/ppermute | solution.py:23
  33.5 5.3 %collective-permute-start.6 = (f32[6,1,130]{2,1,0:T(1,128)S(1)}, f32[6,1,130]{2,1,0:T(1,128)S(1)}, u32[]{:S(2)}, u32[]{:S(2)}) collective-permute-start(f32[6,1,130]{2,1,0:T(1,128)S(1)} %get-tuple-element.23), channel_id=1, source_target_pairs={{0,16},{16,32},{32,48},{48,64},{64,80},{80,96},{96,112},{1,17},{17... | collective-permute-start | bytes 9368 | tf_op jit(solution)/shard_map/ppermute | solution.py:22
  40.3 0.8 copy-start.18
  41.9 1.3 copy-start.4
  43.1 0.8 copy-start.7
  58.8 6.0 %collective-permute-start.8 = (f32[54,16,1]{2,1,0:T(8,128)S(1)}, f32[54,16,1]{2,1,0:T(8,128)S(1)}, u32[]{:S(2)}, u32[]{:S(2)}) collective-permute-start(f32[54,16,1]{2,1,0:T(8,128)S(1)} %get-tuple-element.18), channel_id=1, source_target_pairs={{0,1},{1,2},{2,3},{3,4},{4,5},{5,6},{6,7},{7,8},{8,9},{9,10},{10,1... | collective-permute-start | bytes 10376 | tf_op jit(solution)/shard_map/ppermute | solution.py:22
  58.8 7.7 %collective-permute-start.9 = (f32[54,16,1]{2,1,0:T(8,128)S(1)}, f32[54,16,1]{2,1,0:T(8,128)S(1)}, u32[]{:S(2)}, u32[]{:S(2)}) collective-permute-start(f32[54,16,1]{2,1,0:T(8,128)S(1)} %get-tuple-element.19), channel_id=1, source_target_pairs={{1,0},{2,1},{3,2},{4,3},{5,4},{6,5},{7,6},{8,7},{9,8},{10,9},{11,1... | collective-permute-start | bytes 10376 | tf_op jit(solution)/shard_map/ppermute | solution.py:23
  64.5 9.5 %copy-start.5 = (f32[1,6,16,128]{3,2,1,0:T(8,128)S(1)}, f32[1,6,16,128]{3,2,1,0:T(8,128)}, u32[]{:S(2)}) copy-start(f32[1,6,16,128]{3,2,1,0:T(8,128)} %copy-done.4) | copy-start | bytes 147460
  66.6 1.0 copy-start.2
  67.6 7.3 %copy-start.3 = (f32[54,16,1]{2,1,0:T(8,128)S(1)}, f32[54,16,1]{2,1,0:T(8,128)}, u32[]{:S(2)}) copy-start(f32[54,16,1]{2,1,0:T(8,128)} %copy-done.2) | copy-start | bytes 10372
  67.6 6.7 %collective-permute-start.10 = (f32[54,1,130]{2,1,0:T(1,128)}, f32[54,1,130]{2,1,0:T(1,128)S(1)}, u32[]{:S(2)}, u32[]{:S(2)}) collective-permute-start(f32[54,1,130]{2,1,0:T(1,128)} %get-tuple-element.14), channel_id=1, source_target_pairs={{16,0},{32,16},{48,32},{64,48},{80,64},{96,80},{112,96},{17,1},{33... | collective-permute-start | bytes 84248 | tf_op jit(solution)/shard_map/ppermute | solution.py:23
  69.1 5.2 %copy-start.12 = (f32[128,54]{1,0:T(8,128)S(1)}, f32[128,54]{1,0:T(8,128)}, u32[]{:S(2)}) copy-start(f32[128,54]{1,0:T(8,128)} %fusion.63) | copy-start | bytes 82948
  69.1 5.9 %collective-permute-start.11 = (f32[54,1,130]{2,1,0:T(1,128)}, f32[54,1,130]{2,1,0:T(1,128)}, u32[]{:S(2)}, u32[]{:S(2)}) collective-permute-start(f32[54,1,130]{2,1,0:T(1,128)} %get-tuple-element.15), channel_id=1, source_target_pairs={{0,16},{16,32},{32,48},{48,64},{64,80},{80,96},{96,112},{1,17},{17... | collective-permute-start | bytes 84248 | tf_op jit(solution)/shard_map/ppermute | solution.py:22
  74.2 0.7 copy-start.15
  77.9 0.7 copy-start.10
  79.2 7.3 %copy-start.13 = (f32[16384]{0:T(1024)S(1)}, f32[16384]{0:T(1024)}, u32[]{:S(2)}) copy-start(f32[16384]{0:T(1024)} %convolution_bitcast_fusion.3) | copy-start | bytes 196612
  79.4 8.4 %collective-permute-start.12 = (f32[54,16,1]{2,1,0:T(8,128)S(1)}, f32[54,16,1]{2,1,0:T(8,128)S(1)}, u32[]{:S(2)}, u32[]{:S(2)}) collective-permute-start(f32[54,16,1]{2,1,0:T(8,128)S(1)} %get-tuple-element.16), channel_id=1, source_target_pairs={{0,1},{1,2},{2,3},{3,4},{4,5},{5,6},{6,7},{7,8},{8,9},{9,10},{10,1... | collective-permute-start | bytes 10376 | tf_op jit(solution)/shard_map/ppermute | solution.py:22
  80.3 7.9 %collective-permute-start.13 = (f32[54,16,1]{2,1,0:T(8,128)S(1)}, f32[54,16,1]{2,1,0:T(8,128)S(1)}, u32[]{:S(2)}, u32[]{:S(2)}) collective-permute-start(f32[54,16,1]{2,1,0:T(8,128)S(1)} %get-tuple-element.17), channel_id=1, source_target_pairs={{1,0},{2,1},{3,2},{4,3},{5,4},{6,5},{7,6},{8,7},{9,8},{10,9},{11,1... | collective-permute-start | bytes 10376 | tf_op jit(solution)/shard_map/ppermute | solution.py:23
  88.6 119.1 %collective-permute-start.14 = (f32[54,1,130]{2,1,0:T(1,128)S(1)}, f32[54,1,130]{2,1,0:T(1,128)S(1)}, u32[]{:S(2)}, u32[]{:S(2)}) collective-permute-start(f32[54,1,130]{2,1,0:T(1,128)S(1)} %get-tuple-element.12), channel_id=1, source_target_pairs={{16,0},{32,16},{48,32},{64,48},{80,64},{96,80},{112,96},{17,1},{33... | collective-permute-start | bytes 84248 | tf_op jit(solution)/shard_map/ppermute | solution.py:23
  89.9 117.8 %collective-permute-start.15 = (f32[54,1,130]{2,1,0:T(1,128)S(1)}, f32[54,1,130]{2,1,0:T(1,128)S(1)}, u32[]{:S(2)}, u32[]{:S(2)}) collective-permute-start(f32[54,1,130]{2,1,0:T(1,128)S(1)} %get-tuple-element.13), channel_id=1, source_target_pairs={{0,16},{16,32},{32,48},{48,64},{64,80},{80,96},{96,112},{1,17},{17... | collective-permute-start | bytes 84248 | tf_op jit(solution)/shard_map/ppermute | solution.py:22
  207.0 80.3 %all-reduce.5.cloned.1.call-start = ((), (), s32[]{:S(2)}) async-start(), calls=%async_computation.1 | async-start | bytes 196608 | tf_op jit(solution)/shard_map/psum | solution.py:172
  207.8 83.1 %copy-start.16 = (f32[24064]{0:T(1024)S(1)}, f32[24064]{0:T(1024)}, u32[]{:S(2)}) copy-start(f32[24064]{0:T(1024)} %param.17) | copy-start | bytes 288772
  225.1 65.8 %copy-start.8 = (bf16[128,128]{1,0:T(8,128)(2,1)S(1)}, bf16[128,128]{1,0:T(8,128)(2,1)}, u32[]{:S(2)}) copy-start(bf16[128,128]{1,0:T(8,128)(2,1)} %param.14) | copy-start | bytes 98308
  287.3 3.6 %copy-start.17 = (bf16[6912]{0:T(1024)(128)(2,1)S(1)}, bf16[6912]{0:T(1024)(128)(2,1)}, u32[]{:S(2)}) copy-start(bf16[6912]{0:T(1024)(128)(2,1)} %reshape.86) | copy-start | bytes 41476
Sparse Core Ops, SparseCore 0:
  87.3 118.1 all-reduce.2
  211.0 76.2 all-reduce.4
where the time goes:
time: 306 us; the launch traced here: 300 us
  waiting for transfers between devices  179 us (58%)
  starting transfers between devices  47.2 us (15%)
  local copies, waits for them, and re-layouts  20.1 us (7%)
  between operations  17.7 us (6%)
  blocking collectives  16.4 us (5%)
  other arithmetic  10.5 us (3%)
  matrix products  9.53 us (3%)
    psum x1, waiting for transfers between devices, on_device(): band = lax.psum(local_grad, 'lon')  111 us
    psum x1, waiting for transfers between devices, on_device(): total_grad, band_square = lax.psum((band, jnp.sum(band * band)), 'lat')  62.2 us
    ppermute x8, starting transfers between devices, with_halo(): after = lax.ppermute(first, axis, down)  24.3 us
    ppermute x8, starting transfers between devices, with_halo(): before = lax.ppermute(last, axis, up)  22.8 us
    psum x1, blocking collectives, on_device(): total_grad, band_square = lax.psum((band, jnp.sum(band * band)), 'lat')  16.4 us
    concatenate x2, local copies, waits for them, and re-layouts, backward_block(): jnp.concatenate([blank, spread, blank, spread, direct - 4.0 * spread, spr...  12.4 us
  transfers between devices with their start and end apart: 18, of which 10 were waited for; matrix products, arithmetic and copies ran while one was open for 2% of the time, Pallas kernels for 0%

commit v1 on v0

v1 whole, which is shorter than its diff:
```python
import functools
import math
from types import SimpleNamespace

import jax
import jax.numpy as jnp
from jax import lax
from jax.experimental import pallas as pl
from jax.experimental.pallas import tpu as pltpu
from jax.sharding import PartitionSpec as P

MESH = pl.DeviceIdType.MESH
F32 = jnp.float32
BF16 = jnp.bfloat16

closure_dt = 0.1
learn_rate = 0.1
epsilon = 1e-06
offsets = [(p, q) for p in (-1, 0, 1) for q in (-1, 0, 1)]

FIELDS, ROWS, COLS = 6, 16, 128
HALO = 4
PITCH = COLS + 2 * HALO
EXT = ROWS + 2 * HALO
LANES = 128
TILES = -(-EXT * PITCH // LANES)
FLAT = TILES * LANES
HID = 128
PATCH = 54
DEEP = 80
PARAMS = 24064
NLON, NLAT = 16, 8
CHUNK = 12


def ring(index, step, size):
    return lax.rem(index + step + size, size)


def tile_range(distance):
    low = (HALO - distance) * PITCH // LANES
    high = -(-(HALO + ROWS + distance) * PITCH // LANES)
    if (high - low) % 2:
        low, high = (low, high + 1) if high < TILES else (low - 1, high)
    return low * LANES, high * LANES


def chunks(low, high, size=512):
    return [(start, min(size, high - start)) for start in range(low, high, size)]


def spread_lanes(tile, length):
    return jnp.concatenate([tile] * (length // LANES), axis=1)


def segments(tile):
    found = []
    base = tile * LANES
    for row in range(EXT):
        start = row * PITCH
        for part, low, high in (
            ("left", start, start + HALO),
            ("main", start + HALO, start + HALO + COLS),
            ("right", start + HALO + COLS, start + PITCH),
        ):
            first, end = max(low, base), min(high, base + LANES)
            if first < end:
                found.append((first - base, end - base, row, part))
    return found


def kernel(
    state_hbm,
    diff_hbm,
    mix_ref,
    mask_hbm,
    first_ref,
    second_ref,
    output_ref,
    cot_hbm,
    noise_hbm,
    final_ref,
    adjoint_ref,
    params_ref,
    ratio_ref,
    state_in,
    diff_in,
    mask_in,
    cot_in,
    noise_in,
    load_sem,
    own_a,
    own_b,
    send_north,
    send_south,
    edge,
    from_north,
    from_south,
    edges_in,
    halo_send,
    halo_recv,
    flat_a,
    flat_b,
    own_ref,
    wide_mask,
    wide_diff,
    state_one,
    state_two,
    lap_ref,
    patch_zero,
    patch_one,
    hid_one_zero,
    hid_two_zero,
    hid_one_one,
    hid_two_one,
    back_one,
    back_two,
    out_grad,
    patch_grad,
    adj_one,
    weights_one,
    weights_three,
    base_params,
    grads,
    recv_one,
    recv_two,
    gathered,
    total_ref,
    send_one_sem,
    recv_one_sem,
    send_two_sem,
    recv_two_sem,
    send_three_sem,
    recv_three_sem,
):
    lat = lax.axis_index("lat")
    lon = lax.axis_index("lon")
    north, south = ring(lat, -1, NLAT), ring(lat, 1, NLAT)
    west, east = ring(lon, -1, NLON), ring(lon, 1, NLON)

    barrier = pltpu.get_barrier_semaphore()
    greet = [{"lon": ring(lon, d, NLON)} for d in range(1, NLON)]
    greet += [{"lat": ring(lat, d, NLAT)} for d in range(1, NLAT)]
    greet += [{"lat": a, "lon": b} for a in (north, south) for b in (west, east)]
    for device in greet:
        pl.semaphore_signal(barrier, inc=1, device_id=device, device_id_type=MESH)

    loads = [
        pltpu.make_async_copy(src, dst, load_sem.at[n])
        for n, (src, dst) in enumerate(
            (
                (state_hbm, state_in),
                (mask_hbm, mask_in),
                (diff_hbm, diff_in),
                (cot_hbm, cot_in),
                (noise_hbm, noise_in),
            )
        )
    ]
    for load in loads:
        load.start()

    lane = lax.broadcasted_iota(jnp.int32, (8, LANES), 1)
    sub = lax.broadcasted_iota(jnp.int32, (8, LANES), 0)
    for load in loads[:4]:
        load.wait()

    own_b[...] = jnp.zeros_like(own_b)
    for r in range(ROWS):
        own_a[r, 0:FIELDS, :] = state_in[:, r, :]
        own_a[r, 6:7, :] = mask_in[r : r + 1, :].astype(F32)
        own_a[r, 7:8, :] = diff_in[r : r + 1, :]
        own_b[r, 0:FIELDS, :] = cot_in[:, r, :]
    edge_a = jnp.zeros((8, LANES), F32)
    edge_b = jnp.zeros((8, LANES), F32)
    for r in range(ROWS):
        j = r + HALO
        turn = (j * PITCH + HALO) % LANES
        tile_a = pltpu.roll(own_a[r], turn, 1)
        tile_b = pltpu.roll(own_b[r], turn, 1)
        own_a[r] = tile_a
        own_b[r] = tile_b
        place = (j * PITCH) % LANES
        pick = (lane >= place) & (lane < place + 2 * HALO)
        edge_a = jnp.where(pick, tile_a, edge_a)
        edge_b = jnp.where(pick, tile_b, edge_b)
        if r < HALO:
            send_north[r] = tile_a
        if r < 2:
            send_north[HALO + r] = tile_b
        if r >= ROWS - HALO:
            send_south[r - (ROWS - HALO)] = tile_a
        if r >= ROWS - 2:
            send_south[HALO + r - (ROWS - 2)] = tile_b
    edge[0] = edge_a
    edge[1] = edge_b

    pl.semaphore_wait(barrier, len(greet))

    def halo_copy(n, source, target, device):
        return pltpu.make_async_remote_copy(
            src_ref=source,
            dst_ref=target,
            send_sem=halo_send.at[n],
            recv_sem=halo_recv.at[n],
            device_id=device,
            device_id_type=MESH,
        )

    halos = [
        halo_copy(0, send_north, from_south, {"lat": north}),
        halo_copy(1, send_south, from_north, {"lat": south}),
        halo_copy(2, edge, edges_in.at[0], {"lat": south, "lon": east}),
        halo_copy(3, edge, edges_in.at[1], {"lon": east}),
        halo_copy(4, edge, edges_in.at[2], {"lat": north, "lon": east}),
        halo_copy(5, edge, edges_in.at[3], {"lat": south, "lon": west}),
        halo_copy(6, edge, edges_in.at[4], {"lon": west}),
        halo_copy(7, edge, edges_in.at[5], {"lat": north, "lon": west}),
    ]
    for copy in halos:
        copy.start()

    weights_one[...] = jnp.zeros_like(weights_one)
    weights_one[:, 0:PATCH] = first_ref[...].astype(F32)
    weights_three[...] = jnp.zeros_like(weights_three)
    weights_three[0:FIELDS, :] = output_ref[...].astype(F32)

    def nt(left, right, precision=None):
        return lax.dot_general(
            left, right, (((1,), (1,)), ((), ())), preferred_element_type=F32, precision=precision
        )

    deep_i = lax.broadcasted_iota(jnp.int32, (DEEP, HID), 0)
    deep_j = lax.broadcasted_iota(jnp.int32, (DEEP, HID), 1)
    deep_f = lax.bitwise_and(deep_i, 7)
    picked = (deep_j == 6 * lax.shift_right_logical(deep_i, 3) + deep_f) & (deep_f < 6) & (deep_i < 72)
    select_f = jnp.where(picked, 1.0, 0.0).astype(F32)
    select = select_f.astype(BF16)
    row = lax.broadcasted_iota(jnp.int32, (HID, HID), 0)
    column = lax.broadcasted_iota(jnp.int32, (HID, HID), 1)
    eye = jnp.where(row == column, 1.0, 0.0).astype(BF16)
    plain_one = weights_one[...].astype(BF16)
    w1 = nt(plain_one, select).astype(BF16)
    w1_t = nt(select, plain_one).astype(BF16)
    w2 = second_ref[...]
    w2_t = nt(eye, w2).astype(BF16)
    w3 = weights_three[...].astype(BF16)
    w3_t = nt(eye, w3).astype(BF16)

    turn_of = lax.bitwise_and(row * PATCH, LANES - 1)
    deep_r = lax.broadcasted_iota(jnp.int32, (56, 2 * HID), 0)
    deep_h = lax.broadcasted_iota(jnp.int32, (56, 2 * HID), 1)
    hid_h = lax.bitwise_and(deep_h, HID - 1)
    lands = lax.shift_right_logical(hid_h * PATCH, 7) + lax.shift_right_logical(deep_h, 7)
    gather_rows = jnp.where(lands == deep_r, 1.0, 0.0).astype(F32)

    def flatten_rows(value, exact):
        for bit in range(1, 7):
            moved = pltpu.roll(value, 1 << bit, 1)
            chosen = lax.bitwise_and(lax.shift_right_logical(turn_of, bit), 1) == 1
            value = jnp.where(chosen, moved, value)
        ahead = jnp.where(column >= turn_of, value, 0.0)
        behind = jnp.where(column < turn_of, value, 0.0)
        both = jnp.concatenate([ahead, behind], axis=0)
        if exact:
            return jnp.dot(
                gather_rows, both, preferred_element_type=F32, precision=lax.Precision.HIGHEST
            )
        return jnp.dot(gather_rows.astype(BF16), both.astype(BF16), preferred_element_type=F32)

    base_params[0:56, :] = flatten_rows(weights_one[...], False)
    base_params[54:182, :] = w2.astype(F32)
    base_params[182:188, :] = output_ref[...].astype(F32)

    for t in range(TILES):
        own = jnp.zeros((8, LANES), F32)
        for first, end, j, part in segments(t):
            if part == "main" and HALO <= j < HALO + ROWS:
                own = jnp.where((lane >= first) & (lane < end), 1.0, own)
        own_ref[:, t * LANES : (t + 1) * LANES] = jnp.concatenate([own] * (HID // 8), axis=0).astype(BF16)

    mix_to = []
    mix_from = []
    for g in range(FIELDS):
        to_tile = jnp.zeros((8, LANES), F32)
        from_tile = jnp.zeros((8, LANES), F32)
        for f in range(FIELDS):
            to_tile = jnp.where(sub == f, mix_ref[f, g], to_tile)
            from_tile = jnp.where(sub == f, mix_ref[g, f], from_tile)
        mix_to.append(to_tile)
        mix_from.append(from_tile)

    def mixed(tiles, value):
        length = value.shape[1]
        total = None
        for g in range(FIELDS):
            term = spread_lanes(tiles[g], length) * jnp.broadcast_to(value[g : g + 1, :], (8, length))
            total = term if total is None else total + term
        return total

    for copy in halos:
        copy.wait_recv()

    def top(value):
        return jnp.where(lat > 0, value, 0.0)

    def bottom(value):
        return jnp.where(lat < NLAT - 1, value, 0.0)

    blank = jnp.zeros((8, LANES), F32)
    sides = []
    for which in range(2):
        sides.append(
            {
                "left": (top(edges_in[0, which]), edges_in[1, which], bottom(edges_in[2, which])),
                "right": (top(edges_in[3, which]), edges_in[4, which], bottom(edges_in[5, which])),
            }
        )

    def source(which, j, part):
        if which == 1 and (j < 2 or j >= EXT - 2):
            return blank
        if part != "main":
            return sides[which][part][0 if j < HALO else 1 if j < HALO + ROWS else 2]
        if j < HALO:
            return top(from_north[j if which == 0 else HALO + j - 2])
        if j < HALO + ROWS:
            return (own_a if which == 0 else own_b)[j - HALO]
        return bottom(from_south[(j - HALO - ROWS) if which == 0 else HALO + j - HALO - ROWS])

    for t in range(TILES):
        here = slice(t * LANES, (t + 1) * LANES)
        for which, target in ((0, flat_a), (1, flat_b)):
            value = blank
            for first, end, j, part in segments(t):
                piece = source(which, j, part)
                value = jnp.where((lane >= first) & (lane < end), piece, value)
            target[:, here] = value
            if which == 0:
                wide_mask[:, here] = jnp.broadcast_to(value[6:7, :], (8, LANES))
                wide_diff[:, here] = jnp.broadcast_to(value[7:8, :], (8, LANES))

    def shift(value, amount):
        return pltpu.roll(value, (-amount) % FLAT, 1)

    def make_patch(value, patch_ref):
        blocks = [value if (p, q) == (0, 0) else shift(value, p * PITCH + q) for p, q in offsets]
        for m in range(5):
            after = blocks[2 * m + 1] if m < 4 else jnp.zeros_like(value)
            patch_ref[16 * m : 16 * m + 16, :] = jnp.concatenate([blocks[2 * m], after], axis=0).astype(BF16)
        lap_ref[...] = blocks[1] + blocks[7] + blocks[3] + blocks[5] - 4.0 * value

    def forward(state_ref, patch_ref, one_ref, two_ref, next_ref, low, high, write_low, write_high):
        for start, size in chunks(low, high):
            here = slice(start, start + size)
            one = jnp.tanh(jnp.dot(w1, patch_ref[:, here], preferred_element_type=F32)).astype(BF16)
            one_ref[:, here] = one
            two = jnp.tanh(jnp.dot(w2, one, preferred_element_type=F32)).astype(BF16)
            two_ref[:, here] = two
            tendency = jnp.dot(w3, two, preferred_element_type=F32)[0:8]
            centre = state_ref[:, here]
            update = (
                centre
                + wide_diff[:, here] * lap_ref[:, here]
                + (mixed(mix_to, centre) + closure_dt * tendency)
            )
            next_ref[:, here] = wide_mask[:, here] * update

    state_one[...] = jnp.zeros_like(state_one)
    make_patch(flat_a[...], patch_zero)
    low, high = tile_range(3)
    forward(flat_a, patch_zero, hid_one_zero, hid_two_zero, state_one, low, high, low, high)
    make_patch(state_one[...], patch_one)
    low, high = tile_range(2)
    forward(state_one, patch_one, hid_one_one, hid_two_one, state_two, low, high, low, high)

    def write_rows(source_ref, target_ref):
        for r in range(ROWS):
            start = (r + HALO) * PITCH + HALO
            t, turn = start // LANES, start % LANES
            before = source_ref[:, t * LANES : (t + 1) * LANES]
            after = source_ref[:, (t + 1) * LANES : (t + 2) * LANES]
            value = pltpu.roll(jnp.where(lane >= turn, before, after), (LANES - turn) % LANES, 1)
            target_ref[:, r, :] = value[0:FIELDS]

    grad_low, grad_high = tile_range(0)
    grad_here = slice(grad_low, grad_high)

    def backward(adj_ref, patch_ref, one_ref, two_ref, low, high):
        for start, size in chunks(low, high):
            here = slice(start, start + size)
            masked = wide_mask[:, here] * adj_ref[:, here]
            low_grad = jnp.concatenate([closure_dt * masked, jnp.zeros_like(masked)], axis=0).astype(BF16)
            out_grad[:, here] = low_grad
            two = two_ref[:, here].astype(F32)
            grad_two = (
                jnp.dot(w3_t, low_grad, preferred_element_type=F32) * (1.0 - two * two)
            ).astype(BF16)
            back_two[:, here] = grad_two
            one = one_ref[:, here].astype(F32)
            grad_one = (
                jnp.dot(w2_t, grad_two, preferred_element_type=F32) * (1.0 - one * one)
            ).astype(BF16)
            back_one[:, here] = grad_one
            grad_zero = jnp.dot(w1_t, grad_one, preferred_element_type=F32)
            spread = wide_diff[:, here] * masked
            direct = masked + mixed(mix_from, masked) - 4.0 * spread
            for k in range(9):
                block = grad_zero[8 * k : 8 * k + 8]
                if k == 4:
                    block = block + direct
                elif k % 2:
                    block = block + spread
                patch_grad[8 * k : 8 * k + 8, here] = block
        own = own_ref[:, grad_here]
        grad_first = nt(back_one[:, grad_here], patch_ref[:, grad_here] * own[0:DEEP])
        grad_second = nt(back_two[:, grad_here], one_ref[:, grad_here] * own)
        grad_output = nt(out_grad[:, grad_here] * own[0:16], two_ref[:, grad_here])
        return grad_first, grad_second, grad_output

    def scatter():
        total = None
        for k, (p, q) in enumerate(offsets):
            block = patch_grad[8 * k : 8 * k + 8, :]
            if (p, q) != (0, 0):
                block = shift(block, -(p * PITCH + q))
            total = block if total is None else total + block
        return total

    patch_grad[...] = jnp.zeros_like(patch_grad)
    low, high = tile_range(2)
    late_first, late_second, late_output = backward(flat_b, patch_one, hid_one_one, hid_two_one, low, high)
    adj_one[...] = scatter()
    low, high = tile_range(1)
    first, second, output = backward(adj_one, patch_zero, hid_one_zero, hid_two_zero, low, high)
    first = first + late_first
    second = second + late_second
    output = output + late_output

    narrow = jnp.dot(first, select_f, preferred_element_type=F32, precision=lax.Precision.HIGHEST)
    others = jnp.concatenate([flatten_rows(narrow, True), output[0:8]], axis=0)
    for i in range(NLON):
        grads[i, 0:8, :] = second[8 * i : 8 * i + 8]
        grads[i, 8:12, :] = others[4 * i : 4 * i + 4]

    scatters = []
    for d in range(1, NLON):
        peer = ring(lon, d, NLON)
        copy = pltpu.make_async_remote_copy(
            src_ref=grads.at[peer],
            dst_ref=recv_one.at[d - 1],
            send_sem=send_one_sem.at[d - 1],
            recv_sem=recv_one_sem.at[d - 1],
            device_id={"lon": peer},
            device_id_type=MESH,
        )
        copy.start()
        scatters.append(copy)

    write_rows(state_two, final_ref)
    adj_one[...] = scatter()
    write_rows(adj_one, adjoint_ref)

    band = grads[lon]
    for d in range(1, NLON):
        scatters[d - 1].wait_recv()
        band = band + recv_one[d - 1]
    recv_two[lat] = band

    exchanges = []
    for d in range(1, NLAT):
        peer = ring(lat, d, NLAT)
        copy = pltpu.make_async_remote_copy(
            src_ref=recv_two.at[lat],
            dst_ref=recv_two.at[lat],
            send_sem=send_two_sem.at[d - 1],
            recv_sem=recv_two_sem.at[d - 1],
            device_id={"lat": peer},
            device_id_type=MESH,
        )
        copy.start()
        exchanges.append(copy)
    for copy in exchanges:
        copy.wait_recv()
    total = recv_two[0]
    squares = total * total
    for b in range(1, NLAT):
        value = recv_two[b]
        total = total + value
        squares = squares + value * value
    gathered[lon, 0:CHUNK, :] = total
    gathered[lon, CHUNK:16, :] = jnp.broadcast_to(jnp.sum(squares, axis=0, keepdims=True), (16 - CHUNK, LANES))

    collects = []
    for d in range(1, NLON):
        peer = ring(lon, d, NLON)
        copy = pltpu.make_async_remote_copy(
            src_ref=gathered.at[lon],
            dst_ref=gathered.at[lon],
            send_sem=send_three_sem.at[d - 1],
            recv_sem=recv_three_sem.at[d - 1],
            device_id={"lon": peer},
            device_id_type=MESH,
        )
        copy.start()
        collects.append(copy)
    loads[4].wait()
    for copy in collects:
        copy.wait_recv()

    square_sum = jnp.zeros((CHUNK, LANES), F32)
    band_sum = jnp.zeros((1, LANES), F32)
    for i in range(NLON):
        value = gathered[i, 0:CHUNK, :]
        square_sum = square_sum + value * value
        band_sum = band_sum + gathered[i, CHUNK : CHUNK + 1, :]
        total_ref[54 + 8 * i : 62 + 8 * i, :] = value[0:8]
        if i < 13:
            total_ref[4 * i : 4 * i + 4, :] = value[8:12]
        elif i == 13:
            total_ref[52:54, :] = value[8:10]
        elif i == 14:
            total_ref[182:186, :] = value[8:12]
        else:
            total_ref[186:188, :] = value[8:10]
    grad_square = jnp.sum(square_sum)
    ratio_ref[0] = jnp.sum(band_sum) / (grad_square + epsilon)
    spread_square = jnp.full((1, LANES), grad_square / PARAMS + epsilon, F32)
    scale = learn_rate / jnp.sqrt(spread_square)
    params_ref[...] = base_params[0:188, :] - scale * total_ref[0:188, :] + noise_in[...]

    for copy in halos + scatters + exchanges + collects:
        copy.wait_send()


def on_device(
    initial_state,
    diffusion,
    mixing,
    land_mask,
    first_layer,
    second_layer,
    output_layer,
    cotangent,
    update_noise,
):
    vmem = pltpu.VMEM
    flat8 = vmem((8, FLAT), F32)
    hidden = vmem((HID, FLAT), BF16)
    dma = pltpu.SemaphoreType.DMA
    scratch = [
        vmem((FIELDS, ROWS, COLS), F32),
        vmem((ROWS, COLS), F32),
        vmem((ROWS, COLS), jnp.int32),
        vmem((FIELDS, ROWS, COLS), F32),
        vmem((188, LANES), F32),
        dma((5,)),
        vmem((ROWS, 8, LANES), F32),
        vmem((ROWS, 8, LANES), F32),
        vmem((6, 8, LANES), F32),
        vmem((6, 8, LANES), F32),
        vmem((2, 8, LANES), F32),
        vmem((6, 8, LANES), F32),
        vmem((6, 8, LANES), F32),
        vmem((6, 2, 8, LANES), F32),
        dma((8,)),
        dma((8,)),
        flat8,
        flat8,
        hidden,
        flat8,
        flat8,
        flat8,
        flat8,
        flat8,
        vmem((DEEP, FLAT), BF16),
        vmem((DEEP, FLAT), BF16),
        hidden,
        hidden,
        hidden,
        hidden,
        hidden,
        hidden,
        vmem((16, FLAT), BF16),
        vmem((72, FLAT), F32),
        flat8,
        vmem((HID, LANES), F32),
        vmem((16, LANES), F32),
        vmem((192, LANES), F32),
        vmem((NLON, CHUNK, LANES), F32),
        vmem((NLON - 1, CHUNK, LANES), F32),
        vmem((NLAT, CHUNK, LANES), F32),
        vmem((NLON, 16, LANES), F32),
        vmem((192, LANES), F32),
        dma((NLON - 1,)),
        dma((NLON - 1,)),
        dma((NLAT - 1,)),
        dma((NLAT - 1,)),
        dma((NLON - 1,)),
        dma((NLON - 1,)),
    ]
    hbm = pl.BlockSpec(memory_space=pl.ANY)
    local = pl.BlockSpec(memory_space=pltpu.VMEM)
    scalars = pl.BlockSpec(memory_space=pltpu.SMEM)
    final, adjoint, params, ratio = pl.pallas_call(
        kernel,
        out_shape=(
            jax.ShapeDtypeStruct((FIELDS, ROWS, COLS), F32),
            jax.ShapeDtypeStruct((FIELDS, ROWS, COLS), F32),
            jax.ShapeDtypeStruct((188, LANES), F32),
            jax.ShapeDtypeStruct((1,), F32),
        ),
        in_specs=[hbm, hbm, scalars, hbm, local, local, local, hbm, hbm],
        out_specs=(local, local, local, scalars),
        scratch_shapes=scratch,
        compiler_params=pltpu.CompilerParams(
            collective_id=0, has_side_effects=True, vmem_limit_bytes=40 * 1024 * 1024
        ),
        name="ocean",
    )(
        initial_state,
        diffusion,
        mixing,
        land_mask,
        first_layer,
        second_layer,
        output_layer,
        cotangent,
        update_noise.reshape(188, LANES),
    )
    return final, adjoint, params.reshape(PARAMS), ratio


def solution(mesh):
    placed = (
        P("ens", "lat", "lon"),
        P("lat", "lon"),
        P(),
        P("lat", "lon"),
        P(),
        P(),
        P(),
        P("ens", "lat", "lon"),
        P("ens"),
    )
    return jax.shard_map(
        on_device,
        mesh=mesh,
        in_specs=placed,
        out_specs=(P("ens", "lat", "lon"), P("ens", "lat", "lon"), P("ens"), P("ens")),
        check_vma=False,
    )
```

time: 306 us -> 52.1 us (0.17); the launches traced: 300 us -> 51.7 us
  waiting for transfers between devices: 179 us -> 0 us
  starting transfers between devices: 47.2 us -> 0 us
  Pallas kernels: 0 us -> 43.2 us
  blocking collectives: 16.4 us -> 0 us
  between operations: 17.7 us -> 2.52 us
  local copies, waits for them, and re-layouts: 20.1 us -> 5.94 us
  other arithmetic: 10.5 us -> 0 us
  matrix products: 9.53 us -> 0 us
    psum x2 -> x0, waiting for transfers between devices: 173 us -> none  [the longest x1 111 us: on_device(): band = lax.psum(local_grad, 'lon')]
    ppermute x16 -> x0, starting transfers between devices: 47.2 us -> none  [the longest x8 24.3 us: with_halo(): after = lax.ppermute(first, axis, down)]
    pallas_call x0 -> x1, Pallas kernels: none -> 43.2 us  [on_device(): pl.pallas_call(kernel, out_shape=(jax.ShapeDtypeStruct((FIELDS, ROWS, COL...]
    psum x1 -> x0, blocking collectives: 16.4 us -> none  [on_device(): total_grad, band_square = lax.psum((band, jnp.sum(band * band)), 'lat')]
    concatenate x4 -> x0, local copies, waits for them, and re-layouts: 12.6 us -> none  [the longest x2 12.4 us: backward_block(): jnp.concatenate([blank, spread, blank, spread, direct - 4.0 * spread, spr...]
    dot_general x22 -> x0, matrix products: 9.53 us -> none  [the longest x6 3.27 us: contract_first(): lax.dot_general(left, right, (((0,), (0,)), ((), ())), preferred_element_...]
    ppermute x16 -> x0, waiting for transfers between devices: 5.08 us -> none  [the longest x8 2.66 us: with_halo(): before = lax.ppermute(last, axis, up)]
    add x3 -> x0, other arithmetic: 3.11 us -> none  [the longest x1 1.57 us: on_device(): params - learn_rate * total_grad / jnp.sqrt(grad_square / params_count +...]
  transfers between devices with their start and end apart: 18 -> 0, of which waited for: 10 -> 0; matrix products, arithmetic and copies ran while one was open for 2% -> 0% of each run, Pallas kernels for 0% -> 0%
where the time goes in v1:
time: 52.1 us; the launch traced here: 51.7 us
  Pallas kernels  43.2 us (83%)
  local copies, waits for them, and re-layouts  5.94 us (11%)
  between operations  2.52 us (5%)
    pallas_call x1, Pallas kernels, on_device(): pl.pallas_call(kernel, out_shape=(jax.ShapeDtypeStruct((FIELDS, ROWS, COL...  43.2 us
    unnamed x20, local copies, waits for them, and re-layouts  5.94 us

profile of v1, /device:TPU:1, one launch (start us, length us, event | category | flops | bytes accessed | tf_op | source)
XLA Modules:
  0.0 51.7 jit_solution(3891579982492096043)
XLA Ops:
  0.6 0.0 copy-start.3
  0.6 0.0 copy-start.4
  0.7 0.0 copy-start.6
  0.7 0.0 copy-start.7
  0.7 0.9 %copy.13.first_ref = bf16[128,54]{1,0:T(8,128)(2,1)S(1)} copy(bf16[128,54]{0,1:T(8,128)(2,1)} %param.13) | data formatting | bytes 27648 | tf_op args[4]
  1.5 0.0 copy-done.3
  1.5 0.0 copy-done.4
  1.5 0.0 copy-done.6
  1.5 0.0 copy-done.7
  1.6 0.0 copy-start
  1.6 0.9 %copy-done = f32[24064]{0:T(1024)S(1)} copy-done((f32[24064]{0:T(1024)S(1)}, f32[24064]{0:T(1024)}, u32[]{:S(2)}) %copy-start) | copy-done | bytes 96280
  2.5 0.0 copy-start.1
  2.5 0.8 %copy-done.1 = f32[6,16,128]{2,1,0:T(8,128)S(1)} copy-done((f32[6,16,128]{2,1,0:T(8,128)S(1)}, f32[6,16,128]{2,1,0:T(8,128)}, u32[]{:S(2)}) %copy-start.1) | copy-done | bytes 49176
  3.3 0.0 copy-start.2
  3.3 0.8 %copy-done.2 = f32[6,16,128]{2,1,0:T(8,128)S(1)} copy-done((f32[6,16,128]{2,1,0:T(8,128)S(1)}, f32[6,16,128]{2,1,0:T(8,128)}, u32[]{:S(2)}) %copy-start.2) | copy-done | bytes 49176
  4.1 0.0 copy-start.5
  4.1 0.7 %copy-done.5 = s32[16,128]{1,0:T(8,128)S(1)} copy-done((s32[16,128]{1,0:T(8,128)S(1)}, s32[16,128]{1,0:T(8,128)}, u32[]{:S(2)}) %copy-start.5) | copy-done | bytes 8216
  4.8 43.2 %ocean.1 = (f32[6,16,128]{2,1,0:T(8,128)S(1)}, f32[6,16,128]{2,1,0:T(8,128)S(1)}, f32[188,128]{1,0:T(8,128)S(1)}, f32[1]{0:T(128)}) custom-call(f32[6,16,128]{2,1,0:T(8,128)S(1)} %copy-done.1, f32[16,128]{1,0:T(8,128)S(1)} %copy-done.4, f32[6,6]{1,0:T(8,128)S(1)} %copy-done.6, s32[16,128]{1,0:T(8,128)S(1)} %copy-done.5, bf16[128,54]{1,0:T(8,128)(2,1)S(1)} %copy.13.first_ref, ...), custom_call_target="tpu_custom_call" | custom-call | tf_op jit(solution)/shard_map/ocean/pallas_call | solution.py:605
  48.0 0.6 %copy.18 = f32[6,16,128]{2,1,0:T(8,128)} copy(f32[6,16,128]{2,1,0:T(8,128)S(1)} %get-tuple-element.16) | data formatting | bytes 98304
  48.6 0.6 %copy.19 = f32[6,16,128]{2,1,0:T(8,128)} copy(f32[6,16,128]{2,1,0:T(8,128)S(1)} %get-tuple-element.17) | data formatting | bytes 98304
  49.2 0.6 %copy.20 = f32[24064]{0:T(1024)} copy(f32[24064]{0:T(1024)S(1)} %bitcast.3) | data formatting | bytes 192512
Async XLA Ops:
  0.6 0.9 %copy-start.3 = (bf16[128,128]{1,0:T(8,128)(2,1)S(1)}, bf16[128,128]{1,0:T(8,128)(2,1)}, u32[]{:S(2)}) copy-start(bf16[128,128]{1,0:T(8,128)(2,1)} %second_ref.1) | copy-start | bytes 98308
  0.6 0.9 %copy-start.4 = (f32[16,128]{1,0:T(8,128)S(1)}, f32[16,128]{1,0:T(8,128)}, u32[]{:S(2)}) copy-start(f32[16,128]{1,0:T(8,128)} %diff_hbm.1) | copy-start | bytes 24580
  0.7 0.9 %copy-start.6 = (f32[6,6]{1,0:T(8,128)S(1)}, f32[6,6]{1,0:T(8,128)}, u32[]{:S(2)}) copy-start(f32[6,6]{1,0:T(8,128)} %mix_ref.1) | copy-start | bytes 436
  0.7 0.9 %copy-start.7 = (bf16[6,128]{1,0:T(8,128)(2,1)S(1)}, bf16[6,128]{1,0:T(8,128)(2,1)}, u32[]{:S(2)}) copy-start(bf16[6,128]{1,0:T(8,128)(2,1)} %output_ref.1) | copy-start | bytes 4612
  1.6 0.9 %copy-start = (f32[24064]{0:T(1024)S(1)}, f32[24064]{0:T(1024)}, u32[]{:S(2)}) copy-start(f32[24064]{0:T(1024)} %param.17) | copy-start | bytes 288772
  2.5 0.8 %copy-start.1 = (f32[6,16,128]{2,1,0:T(8,128)S(1)}, f32[6,16,128]{2,1,0:T(8,128)}, u32[]{:S(2)}) copy-start(f32[6,16,128]{2,1,0:T(8,128)} %state_hbm.1) | copy-start | bytes 147460
  3.3 0.8 %copy-start.2 = (f32[6,16,128]{2,1,0:T(8,128)S(1)}, f32[6,16,128]{2,1,0:T(8,128)}, u32[]{:S(2)}) copy-start(f32[6,16,128]{2,1,0:T(8,128)} %cot_hbm.1) | copy-start | bytes 147460
  4.1 0.7 %copy-start.5 = (s32[16,128]{1,0:T(8,128)S(1)}, s32[16,128]{1,0:T(8,128)}, u32[]{:S(2)}) copy-start(s32[16,128]{1,0:T(8,128)} %mask_hbm.1) | copy-start | bytes 24580

commit v2 on v1

--- a/solution.py
+++ b/solution.py
@@ -72,11 +72,11 @@
 def kernel(
     state_hbm,
     diff_hbm,
-    mix_ref,
+    mix_hbm,
     mask_hbm,
-    first_ref,
-    second_ref,
-    output_ref,
+    first_hbm,
+    second_hbm,
+    output_hbm,
     cot_hbm,
     noise_hbm,
     final_ref,
@@ -88,6 +88,10 @@
     mask_in,
     cot_in,
     noise_in,
+    mix_ref,
+    first_ref,
+    second_ref,
+    output_ref,
     load_sem,
     own_a,
     own_b,
@@ -153,6 +157,10 @@
                 (mask_hbm, mask_in),
                 (diff_hbm, diff_in),
                 (cot_hbm, cot_in),
+                (mix_hbm, mix_ref),
+                (first_hbm, first_ref),
+                (second_hbm, second_ref),
+                (output_hbm, output_ref),
                 (noise_hbm, noise_in),
             )
         )
@@ -220,8 +228,10 @@
     for copy in halos:
         copy.start()
 
+    for load in loads[4:8]:
+        load.wait()
     weights_one[...] = jnp.zeros_like(weights_one)
-    weights_one[:, 0:PATCH] = first_ref[...].astype(F32)
+    weights_one[0:PATCH, :] = first_ref[...].astype(F32)
     weights_three[...] = jnp.zeros_like(weights_three)
     weights_three[0:FIELDS, :] = output_ref[...].astype(F32)
 
@@ -239,9 +249,10 @@
     row = lax.broadcasted_iota(jnp.int32, (HID, HID), 0)
     column = lax.broadcasted_iota(jnp.int32, (HID, HID), 1)
     eye = jnp.where(row == column, 1.0, 0.0).astype(BF16)
-    plain_one = weights_one[...].astype(BF16)
+    turned_one = weights_one[...].astype(BF16)
+    plain_one = nt(eye, turned_one).astype(BF16)
     w1 = nt(plain_one, select).astype(BF16)
-    w1_t = nt(select, plain_one).astype(BF16)
+    w1_t = jnp.dot(select, turned_one, preferred_element_type=F32).astype(BF16)
     w2 = second_ref[...]
     w2_t = nt(eye, w2).astype(BF16)
     w3 = weights_three[...].astype(BF16)
@@ -268,7 +279,7 @@
             )
         return jnp.dot(gather_rows.astype(BF16), both.astype(BF16), preferred_element_type=F32)
 
-    base_params[0:56, :] = flatten_rows(weights_one[...], False)
+    base_params[0:56, :] = flatten_rows(plain_one.astype(F32), False)
     base_params[54:182, :] = w2.astype(F32)
     base_params[182:188, :] = output_ref[...].astype(F32)
 
@@ -504,7 +515,7 @@
         )
         copy.start()
         collects.append(copy)
-    loads[4].wait()
+    loads[8].wait()
     for copy in collects:
         copy.wait_recv()
 
@@ -524,13 +535,23 @@
         else:
             total_ref[186:188, :] = value[8:10]
     grad_square = jnp.sum(square_sum)
-    ratio_ref[0] = jnp.sum(band_sum) / (grad_square + epsilon)
+    ratio_ref[...] = jnp.full((1, LANES), jnp.sum(band_sum) / (grad_square + epsilon), F32)
     spread_square = jnp.full((1, LANES), grad_square / PARAMS + epsilon, F32)
     scale = learn_rate / jnp.sqrt(spread_square)
     params_ref[...] = base_params[0:188, :] - scale * total_ref[0:188, :] + noise_in[...]
 
     for copy in halos + scatters + exchanges + collects:
         copy.wait_send()
+
+
+def emit(final_in, adjoint_in, params_in, ratio_in, final_out, adjoint_out, params_out, ratio_out, sem):
+    pairs = ((final_in, final_out), (adjoint_in, adjoint_out), (params_in, params_out))
+    copies = [pltpu.make_async_copy(src, dst, sem.at[n]) for n, (src, dst) in enumerate(pairs)]
+    for copy in copies:
+        copy.start()
+    ratio_out[0] = ratio_in[0, 0]
+    for copy in copies:
+        copy.wait()
 
 
 def on_device(
@@ -554,7 +575,11 @@
         vmem((ROWS, COLS), jnp.int32),
         vmem((FIELDS, ROWS, COLS), F32),
         vmem((188, LANES), F32),
-        dma((5,)),
+        pltpu.SMEM((FIELDS, FIELDS), F32),
+        vmem((PATCH, HID), BF16),
+        vmem((HID, HID), BF16),
+        vmem((FIELDS, HID), BF16),
+        dma((9,)),
         vmem((ROWS, 8, LANES), F32),
         vmem((ROWS, 8, LANES), F32),
         vmem((6, 8, LANES), F32),
@@ -599,35 +624,52 @@
         dma((NLON - 1,)),
         dma((NLON - 1,)),
     ]
-    hbm = pl.BlockSpec(memory_space=pl.ANY)
+    hbm = pl.BlockSpec(memory_space=pltpu.HBM)
     local = pl.BlockSpec(memory_space=pltpu.VMEM)
-    scalars = pl.BlockSpec(memory_space=pltpu.SMEM)
     final, adjoint, params, ratio = pl.pallas_call(
         kernel,
         out_shape=(
             jax.ShapeDtypeStruct((FIELDS, ROWS, COLS), F32),
             jax.ShapeDtypeStruct((FIELDS, ROWS, COLS), F32),
             jax.ShapeDtypeStruct((188, LANES), F32),
-            jax.ShapeDtypeStruct((1,), F32),
+            jax.ShapeDtypeStruct((1, LANES), F32),
         ),
-        in_specs=[hbm, hbm, scalars, hbm, local, local, local, hbm, hbm],
-        out_specs=(local, local, local, scalars),
+        in_specs=[hbm] * 9,
+        out_specs=(local,) * 4,
         scratch_shapes=scratch,
         compiler_params=pltpu.CompilerParams(
             collective_id=0, has_side_effects=True, vmem_limit_bytes=40 * 1024 * 1024
         ),
         name="ocean",
     )(
-        initial_state,
-        diffusion,
-        mixing,
-        land_mask,
-        first_layer,
-        second_layer,
-        output_layer,
-        cotangent,
-        update_noise.reshape(188, LANES),
+        *(
+            pltpu.with_memory_space_constraint(value, pltpu.HBM)
+            for value in (
+                initial_state,
+                diffusion,
+                mixing,
+                land_mask,
+                first_layer.T,
+                second_layer,
+                output_layer,
+                cotangent,
+                update_noise.reshape(188, LANES),
+            )
+        )
     )
+    final, adjoint, params, ratio = pl.pallas_call(
+        emit,
+        out_shape=(
+            jax.ShapeDtypeStruct((FIELDS, ROWS, COLS), F32),
+            jax.ShapeDtypeStruct((FIELDS, ROWS, COLS), F32),
+            jax.ShapeDtypeStruct((188, LANES), F32),
+            jax.ShapeDtypeStruct((1,), F32),
+        ),
+        in_specs=[local] * 4,
+        out_specs=(hbm, hbm, hbm, pl.BlockSpec(memory_space=pltpu.SMEM)),
+        scratch_shapes=[dma((3,))],
+        name="emit",
+    )(*(pltpu.with_memory_space_constraint(value, pltpu.VMEM) for value in (final, adjoint, params, ratio)))
     return final, adjoint, params.reshape(PARAMS), ratio
 
 

time: 52.1 us -> 44.2 us (0.85)
  local copies, waits for them, and re-layouts: 5.94 us -> 0 us
  between operations: 2.52 us -> 0.64 us
    unnamed x20 -> x0, local copies, waits for them, and re-layouts: 5.94 us -> none
    pallas_call x0 -> x1, Pallas kernels: none -> 1.22 us  [on_device(): pl.pallas_call(emit, out_shape=(jax.ShapeDtypeStruct((FIELDS, ROWS, COLS)...]
    pallas_call x1, Pallas kernels: 43.2 us -> 42.2 us  [on_device(): pl.pallas_call(kernel, out_shape=(jax.ShapeDtypeStruct((FIELDS, ROWS, COL...]
where the time goes in v2:
time: 44.2 us; the launch traced here: 44 us
  Pallas kernels  43.4 us (98%)
  between operations  0.64 us (1%)
    pallas_call x1, Pallas kernels, on_device(): pl.pallas_call(kernel, out_shape=(jax.ShapeDtypeStruct((FIELDS, ROWS, COL...  42.2 us
    pallas_call x1, Pallas kernels, on_device(): pl.pallas_call(emit, out_shape=(jax.ShapeDtypeStruct((FIELDS, ROWS, COLS)...  1.22 us

profile of v2, /device:TPU:1, one launch (start us, length us, event | category | flops | bytes accessed | tf_op | source)
XLA Modules:
  0.0 44.0 jit_solution(4100930513779661820)
XLA Ops:
  0.6 42.2 %ocean.1 = (f32[6,16,128]{2,1,0:T(8,128)S(1)}, f32[6,16,128]{2,1,0:T(8,128)S(1)}, f32[188,128]{1,0:T(8,128)S(1)}, f32[1,128]{1,0:T(1,128)S(1)}) custom-call(f32[6,16,128]{2,1,0:T(8,128)} %state_hbm.1, f32[16,128]{1,0:T(8,128)} %diff_hbm.1, f32[6,6]{1,0:T(8,128)} %mix_hbm.1, s32[16,128]{1,0:T(8,128)} %mask_hbm.1, bf16[54,128]{1,0:T(8,128)(2,1)} %bitcast.4, ...), custom_call_target="tpu_custom_call" | custom-call | tf_op jit(solution)/shard_map/ocean/pallas_call | solution.py:629
  42.8 1.2 %emit.1 = (f32[6,16,128]{2,1,0:T(8,128)}, f32[6,16,128]{2,1,0:T(8,128)}, f32[188,128]{1,0:T(8,128)}, f32[1]{0:T(128)}) custom-call(f32[6,16,128]{2,1,0:T(8,128)S(1)} %get-tuple-element.12.final_in, f32[6,16,128]{2,1,0:T(8,128)S(1)} %get-tuple-element.13.adjoint_in, f32[188,128]{1,0:T(8,128)S(1)} %get-tuple-element.14.params_in, ...), custom_call_target="tpu_custom_call" | custom-call | tf_op jit(solution)/shard_map/emit/pallas_call | solution.py:660

commit v3 on v2

--- a/solution.py
+++ b/solution.py
@@ -45,7 +45,7 @@
     return low * LANES, high * LANES
 
 
-def chunks(low, high, size=512):
+def chunks(low, high, size=4096):
     return [(start, min(size, high - start)) for start in range(low, high, size)]
 
 

time: 44.2 us -> 39.1 us (0.88)
  Pallas kernels: 43.4 us -> 38.3 us
    pallas_call x1, Pallas kernels: 42.2 us -> 37.1 us  [on_device(): pl.pallas_call(kernel, out_shape=(jax.ShapeDtypeStruct((FIELDS, ROWS, COL...]
where the time goes in v3:
time: 39.1 us; the launch traced here: 39 us
  Pallas kernels  38.3 us (98%)
  between operations  0.64 us (2%)
    pallas_call x1, Pallas kernels, on_device(): pl.pallas_call(kernel, out_shape=(jax.ShapeDtypeStruct((FIELDS, ROWS, COL...  37.1 us
    pallas_call x1, Pallas kernels, on_device(): pl.pallas_call(emit, out_shape=(jax.ShapeDtypeStruct((FIELDS, ROWS, COLS)...  1.22 us

profile of v3, /device:TPU:1, one launch (start us, length us, event | category | flops | bytes accessed | tf_op | source)
XLA Modules:
  0.0 39.0 jit_solution(4818434782890821470)
XLA Ops:
  0.6 37.1 %ocean.1 = (f32[6,16,128]{2,1,0:T(8,128)S(1)}, f32[6,16,128]{2,1,0:T(8,128)S(1)}, f32[188,128]{1,0:T(8,128)S(1)}, f32[1,128]{1,0:T(1,128)S(1)}) custom-call(f32[6,16,128]{2,1,0:T(8,128)} %state_hbm.1, f32[16,128]{1,0:T(8,128)} %diff_hbm.1, f32[6,6]{1,0:T(8,128)} %mix_hbm.1, s32[16,128]{1,0:T(8,128)} %mask_hbm.1, bf16[54,128]{1,0:T(8,128)(2,1)} %bitcast.4, ...), custom_call_target="tpu_custom_call" | custom-call | tf_op jit(solution)/shard_map/ocean/pallas_call | solution.py:629
  37.8 1.2 %emit.1 = (f32[6,16,128]{2,1,0:T(8,128)}, f32[6,16,128]{2,1,0:T(8,128)}, f32[188,128]{1,0:T(8,128)}, f32[1]{0:T(128)}) custom-call(f32[6,16,128]{2,1,0:T(8,128)S(1)} %get-tuple-element.12.final_in, f32[6,16,128]{2,1,0:T(8,128)S(1)} %get-tuple-element.13.adjoint_in, f32[188,128]{1,0:T(8,128)S(1)} %get-tuple-element.14.params_in, ...), custom_call_target="tpu_custom_call" | custom-call | tf_op jit(solution)/shard_map/emit/pallas_call | solution.py:660

commit v4 on v3

--- a/solution.py
+++ b/solution.py
@@ -31,6 +31,9 @@
 PARAMS = 24064
 NLON, NLAT = 16, 8
 CHUNK = 12
+SENT = CHUNK + 1
+LON_STEPS = (8, 7, 9, 6, 10, 5, 11, 4, 12, 3, 13, 2, 14, 1, 15)
+LAT_STEPS = (2, 6, 1, 3, 5, 7, 4)
 
 
 def ring(index, step, size):
@@ -98,11 +101,9 @@
     send_north,
     send_south,
     edge,
-    from_north,
-    from_south,
-    edges_in,
-    halo_send,
-    halo_recv,
+    halo_in,
+    send_sem,
+    recv_sem,
     flat_a,
     flat_b,
     own_ref,
@@ -130,12 +131,6 @@
     recv_two,
     gathered,
     total_ref,
-    send_one_sem,
-    recv_one_sem,
-    send_two_sem,
-    recv_two_sem,
-    send_three_sem,
-    recv_three_sem,
 ):
     lat = lax.axis_index("lat")
     lon = lax.axis_index("lon")
@@ -143,9 +138,10 @@
     west, east = ring(lon, -1, NLON), ring(lon, 1, NLON)
 
     barrier = pltpu.get_barrier_semaphore()
-    greet = [{"lon": ring(lon, d, NLON)} for d in range(1, NLON)]
-    greet += [{"lat": ring(lat, d, NLAT)} for d in range(1, NLAT)]
-    greet += [{"lat": a, "lon": b} for a in (north, south) for b in (west, east)]
+    corners = [{"lat": a, "lon": b} for a in (north, south) for b in (west, east)]
+    greet = [{"lon": ring(lon, d, NLON)} for d in LON_STEPS[:5]] + corners
+    greet += [{"lat": ring(lat, d, NLAT)} for d in LAT_STEPS]
+    greet += [{"lon": ring(lon, d, NLON)} for d in LON_STEPS[5:]]
     for device in greet:
         pl.semaphore_signal(barrier, inc=1, device_id=device, device_id_type=MESH)
 
@@ -205,25 +201,27 @@
 
     pl.semaphore_wait(barrier, len(greet))
 
-    def halo_copy(n, source, target, device):
+    def halo_copy(source, target, device):
         return pltpu.make_async_remote_copy(
             src_ref=source,
             dst_ref=target,
-            send_sem=halo_send.at[n],
-            recv_sem=halo_recv.at[n],
+            send_sem=send_sem.at[0],
+            recv_sem=recv_sem.at[0],
             device_id=device,
             device_id_type=MESH,
         )
 
+    from_north, from_south = halo_in.at[0:6], halo_in.at[6:12]
+    edges_in = [halo_in.at[12 + 2 * n : 14 + 2 * n] for n in range(6)]
     halos = [
-        halo_copy(0, send_north, from_south, {"lat": north}),
-        halo_copy(1, send_south, from_north, {"lat": south}),
-        halo_copy(2, edge, edges_in.at[0], {"lat": south, "lon": east}),
-        halo_copy(3, edge, edges_in.at[1], {"lon": east}),
-        halo_copy(4, edge, edges_in.at[2], {"lat": north, "lon": east}),
-        halo_copy(5, edge, edges_in.at[3], {"lat": south, "lon": west}),
-        halo_copy(6, edge, edges_in.at[4], {"lon": west}),
-        halo_copy(7, edge, edges_in.at[5], {"lat": north, "lon": west}),
+        halo_copy(edge, edges_in[0], {"lat": south, "lon": east}),
+        halo_copy(edge, edges_in[2], {"lat": north, "lon": east}),
+        halo_copy(edge, edges_in[3], {"lat": south, "lon": west}),
+        halo_copy(edge, edges_in[5], {"lat": north, "lon": west}),
+        halo_copy(send_north, from_south, {"lat": north}),
+        halo_copy(send_south, from_north, {"lat": south}),
+        halo_copy(edge, edges_in[1], {"lon": east}),
+        halo_copy(edge, edges_in[4], {"lon": west}),
     ]
     for copy in halos:
         copy.start()
@@ -244,8 +242,7 @@
     deep_j = lax.broadcasted_iota(jnp.int32, (DEEP, HID), 1)
     deep_f = lax.bitwise_and(deep_i, 7)
     picked = (deep_j == 6 * lax.shift_right_logical(deep_i, 3) + deep_f) & (deep_f < 6) & (deep_i < 72)
-    select_f = jnp.where(picked, 1.0, 0.0).astype(F32)
-    select = select_f.astype(BF16)
+    select = jnp.where(picked, 1.0, 0.0).astype(BF16)
     row = lax.broadcasted_iota(jnp.int32, (HID, HID), 0)
     column = lax.broadcasted_iota(jnp.int32, (HID, HID), 1)
     eye = jnp.where(row == column, 1.0, 0.0).astype(BF16)
@@ -263,21 +260,31 @@
     deep_h = lax.broadcasted_iota(jnp.int32, (56, 2 * HID), 1)
     hid_h = lax.bitwise_and(deep_h, HID - 1)
     lands = lax.shift_right_logical(hid_h * PATCH, 7) + lax.shift_right_logical(deep_h, 7)
-    gather_rows = jnp.where(lands == deep_r, 1.0, 0.0).astype(F32)
+    gather_rows = jnp.where(lands == deep_r, 1.0, 0.0).astype(BF16)
+
+    def halves(value):
+        high = value.astype(BF16)
+        return high, (value - high.astype(F32)).astype(BF16)
 
     def flatten_rows(value, exact):
-        for bit in range(1, 7):
-            moved = pltpu.roll(value, 1 << bit, 1)
-            chosen = lax.bitwise_and(lax.shift_right_logical(turn_of, bit), 1) == 1
-            value = jnp.where(chosen, moved, value)
+        turned = []
+        for m in range(HID // 8):
+            tile = value[8 * m : 8 * m + 8]
+            if (8 * m * PATCH) % LANES:
+                tile = pltpu.roll(tile, (8 * m * PATCH) % LANES, 1)
+            for _ in range(3):
+                tile = pltpu.roll(tile, 0, 1, stride=PATCH // 3, stride_axis=0)
+            turned.append(tile)
+        value = jnp.concatenate(turned, axis=0)
         ahead = jnp.where(column >= turn_of, value, 0.0)
         behind = jnp.where(column < turn_of, value, 0.0)
         both = jnp.concatenate([ahead, behind], axis=0)
-        if exact:
-            return jnp.dot(
-                gather_rows, both, preferred_element_type=F32, precision=lax.Precision.HIGHEST
-            )
-        return jnp.dot(gather_rows.astype(BF16), both.astype(BF16), preferred_element_type=F32)
+        if not exact:
+            return jnp.dot(gather_rows, both.astype(BF16), preferred_element_type=F32)
+        high, low = halves(both)
+        return jnp.dot(gather_rows, high, preferred_element_type=F32) + jnp.dot(
+            gather_rows, low, preferred_element_type=F32
+        )
 
     base_params[0:56, :] = flatten_rows(plain_one.astype(F32), False)
     base_params[54:182, :] = w2.astype(F32)
@@ -309,8 +316,8 @@
             total = term if total is None else total + term
         return total
 
-    for copy in halos:
-        copy.wait_recv()
+    all_halos = halo_copy(halo_in, halo_in, {"lon": east})
+    all_halos.wait_recv()
 
     def top(value):
         return jnp.where(lat > 0, value, 0.0)
@@ -323,8 +330,8 @@
     for which in range(2):
         sides.append(
             {
-                "left": (top(edges_in[0, which]), edges_in[1, which], bottom(edges_in[2, which])),
-                "right": (top(edges_in[3, which]), edges_in[4, which], bottom(edges_in[5, which])),
+                "left": (top(halo_in[12 + which]), halo_in[14 + which], bottom(halo_in[16 + which])),
+                "right": (top(halo_in[18 + which]), halo_in[20 + which], bottom(halo_in[22 + which])),
             }
         )
 
@@ -334,10 +341,10 @@
         if part != "main":
             return sides[which][part][0 if j < HALO else 1 if j < HALO + ROWS else 2]
         if j < HALO:
-            return top(from_north[j if which == 0 else HALO + j - 2])
+            return top(halo_in[j if which == 0 else HALO + j - 2])
         if j < HALO + ROWS:
             return (own_a if which == 0 else own_b)[j - HALO]
-        return bottom(from_south[(j - HALO - ROWS) if which == 0 else HALO + j - HALO - ROWS])
+        return bottom(halo_in[6 + (j - HALO - ROWS if which == 0 else j - ROWS)])
 
     for t in range(TILES):
         here = slice(t * LANES, (t + 1) * LANES)
@@ -448,51 +455,58 @@
     second = second + late_second
     output = output + late_output
 
-    narrow = jnp.dot(first, select_f, preferred_element_type=F32, precision=lax.Precision.HIGHEST)
+    high_part, low_part = halves(first)
+    narrow = jnp.dot(high_part, select, preferred_element_type=F32) + jnp.dot(
+        low_part, select, preferred_element_type=F32
+    )
     others = jnp.concatenate([flatten_rows(narrow, True), output[0:8]], axis=0)
     for i in range(NLON):
         grads[i, 0:8, :] = second[8 * i : 8 * i + 8]
         grads[i, 8:12, :] = others[4 * i : 4 * i + 4]
 
-    scatters = []
-    for d in range(1, NLON):
-        peer = ring(lon, d, NLON)
-        copy = pltpu.make_async_remote_copy(
-            src_ref=grads.at[peer],
-            dst_ref=recv_one.at[d - 1],
-            send_sem=send_one_sem.at[d - 1],
-            recv_sem=recv_one_sem.at[d - 1],
-            device_id={"lon": peer},
+    def copies_along(axis, here, steps, size, phase, source, target):
+        made = []
+        for place, d in enumerate(steps):
+            peer = ring(here, d, size)
+            made.append(
+                pltpu.make_async_remote_copy(
+                    src_ref=source(peer),
+                    dst_ref=target(place),
+                    send_sem=send_sem.at[phase],
+                    recv_sem=recv_sem.at[phase],
+                    device_id={axis: peer},
+                    device_id_type=MESH,
+                )
+            )
+        for copy in made:
+            copy.start()
+
+    def all_of(phase, buffer):
+        return pltpu.make_async_remote_copy(
+            src_ref=buffer,
+            dst_ref=buffer,
+            send_sem=send_sem.at[phase],
+            recv_sem=recv_sem.at[phase],
+            device_id={"lon": east},
             device_id_type=MESH,
         )
-        copy.start()
-        scatters.append(copy)
+
+    copies_along("lon", lon, LON_STEPS, NLON, 1, lambda peer: grads.at[peer], lambda place: recv_one.at[place])
 
     write_rows(state_two, final_ref)
     adj_one[...] = scatter()
     write_rows(adj_one, adjoint_ref)
 
+    scatters = all_of(1, recv_one)
+    scatters.wait_recv()
     band = grads[lon]
-    for d in range(1, NLON):
-        scatters[d - 1].wait_recv()
-        band = band + recv_one[d - 1]
+    for n in range(NLON - 1):
+        band = band + recv_one[n]
     recv_two[lat] = band
 
-    exchanges = []
-    for d in range(1, NLAT):
-        peer = ring(lat, d, NLAT)
-        copy = pltpu.make_async_remote_copy(
-            src_ref=recv_two.at[lat],
-            dst_ref=recv_two.at[lat],
-            send_sem=send_two_sem.at[d - 1],
-            recv_sem=recv_two_sem.at[d - 1],
-            device_id={"lat": peer},
-            device_id_type=MESH,
-        )
-        copy.start()
-        exchanges.append(copy)
-    for copy in exchanges:
-        copy.wait_recv()
+    copies_along("lat", lat, LAT_STEPS, NLAT, 2, lambda peer: recv_two.at[lat], lambda place: recv_two.at[lat])
+    exchanges = all_of(2, recv_two.at[0 : NLAT - 1])
+    exchanges.wait_recv()
     total = recv_two[0]
     squares = total * total
     for b in range(1, NLAT):
@@ -500,24 +514,12 @@
         total = total + value
         squares = squares + value * value
     gathered[lon, 0:CHUNK, :] = total
-    gathered[lon, CHUNK:16, :] = jnp.broadcast_to(jnp.sum(squares, axis=0, keepdims=True), (16 - CHUNK, LANES))
-
-    collects = []
-    for d in range(1, NLON):
-        peer = ring(lon, d, NLON)
-        copy = pltpu.make_async_remote_copy(
-            src_ref=gathered.at[lon],
-            dst_ref=gathered.at[lon],
-            send_sem=send_three_sem.at[d - 1],
-            recv_sem=recv_three_sem.at[d - 1],
-            device_id={"lon": peer},
-            device_id_type=MESH,
-        )
-        copy.start()
-        collects.append(copy)
+    gathered[lon, CHUNK:SENT, :] = jnp.sum(squares, axis=0, keepdims=True)
+
+    copies_along("lon", lon, LON_STEPS, NLON, 3, lambda peer: gathered.at[lon], lambda place: gathered.at[lon])
     loads[8].wait()
-    for copy in collects:
-        copy.wait_recv()
+    collects = all_of(3, gathered.at[0 : NLON - 1])
+    collects.wait_recv()
 
     square_sum = jnp.zeros((CHUNK, LANES), F32)
     band_sum = jnp.zeros((1, LANES), F32)
@@ -540,16 +542,18 @@
     scale = learn_rate / jnp.sqrt(spread_square)
     params_ref[...] = base_params[0:188, :] - scale * total_ref[0:188, :] + noise_in[...]
 
-    for copy in halos + scatters + exchanges + collects:
-        copy.wait_send()
-
-
-def emit(final_in, adjoint_in, params_in, ratio_in, final_out, adjoint_out, params_out, ratio_out, sem):
+    for copies in (all_halos, scatters, exchanges, collects):
+        copies.wait_send()
+
+
+def emit(final_in, adjoint_in, params_in, ratio_in, final_out, adjoint_out, params_out, ratio_out, held, sem):
     pairs = ((final_in, final_out), (adjoint_in, adjoint_out), (params_in, params_out))
     copies = [pltpu.make_async_copy(src, dst, sem.at[n]) for n, (src, dst) in enumerate(pairs)]
     for copy in copies:
         copy.start()
-    ratio_out[0] = ratio_in[0, 0]
+    held[0] = ratio_in[0, 0]
+    copies.append(pltpu.make_async_copy(held, ratio_out, sem.at[3]))
+    copies[3].start()
     for copy in copies:
         copy.wait()
 
@@ -585,11 +589,9 @@
         vmem((6, 8, LANES), F32),
         vmem((6, 8, LANES), F32),
         vmem((2, 8, LANES), F32),
-        vmem((6, 8, LANES), F32),
-        vmem((6, 8, LANES), F32),
-        vmem((6, 2, 8, LANES), F32),
-        dma((8,)),
-        dma((8,)),
+        vmem((24, 8, LANES), F32),
+        dma((4,)),
+        dma((4,)),
         flat8,
         flat8,
         hidden,
@@ -615,14 +617,8 @@
         vmem((NLON, CHUNK, LANES), F32),
         vmem((NLON - 1, CHUNK, LANES), F32),
         vmem((NLAT, CHUNK, LANES), F32),
-        vmem((NLON, 16, LANES), F32),
+        vmem((NLON, SENT, LANES), F32),
         vmem((192, LANES), F32),
-        dma((NLON - 1,)),
-        dma((NLON - 1,)),
-        dma((NLAT - 1,)),
-        dma((NLAT - 1,)),
-        dma((NLON - 1,)),
-        dma((NLON - 1,)),
     ]
     hbm = pl.BlockSpec(memory_space=pltpu.HBM)
     local = pl.BlockSpec(memory_space=pltpu.VMEM)
@@ -666,8 +662,8 @@
             jax.ShapeDtypeStruct((1,), F32),
         ),
         in_specs=[local] * 4,
-        out_specs=(hbm, hbm, hbm, pl.BlockSpec(memory_space=pltpu.SMEM)),
-        scratch_shapes=[dma((3,))],
+        out_specs=(hbm,) * 4,
+        scratch_shapes=[pltpu.SMEM((1,), F32), dma((4,))],
         name="emit",
     )(*(pltpu.with_memory_space_constraint(value, pltpu.VMEM) for value in (final, adjoint, params, ratio)))
     return final, adjoint, params.reshape(PARAMS), ratio

time: 39.1 us -> 36.4 us (0.931)
  Pallas kernels: 38.3 us -> 35.6 us
    pallas_call x1, Pallas kernels: 37.1 us -> 34.9 us  [on_device(): pl.pallas_call(kernel, out_shape=(jax.ShapeDtypeStruct((FIELDS, ROWS, COL...]
    pallas_call x1, Pallas kernels: 1.22 us -> 0.72 us  [on_device(): pl.pallas_call(emit, out_shape=(jax.ShapeDtypeStruct((FIELDS, ROWS, COLS)...]
where the time goes in v4:
time: 36.4 us; the launch traced here: 36.3 us
  Pallas kernels  35.6 us (98%)
  between operations  0.64 us (2%)
    pallas_call x1, Pallas kernels, on_device(): pl.pallas_call(kernel, out_shape=(jax.ShapeDtypeStruct((FIELDS, ROWS, COL...  34.9 us

profile of v4, /device:TPU:1, one launch (start us, length us, event | category | flops | bytes accessed | tf_op | source)
XLA Modules:
  0.0 36.3 jit_solution(1299099274199985038)
XLA Ops:
  0.6 34.9 %ocean.1 = (f32[6,16,128]{2,1,0:T(8,128)S(1)}, f32[6,16,128]{2,1,0:T(8,128)S(1)}, f32[188,128]{1,0:T(8,128)S(1)}, f32[1,128]{1,0:T(1,128)S(1)}) custom-call(f32[6,16,128]{2,1,0:T(8,128)} %state_hbm.1, f32[16,128]{1,0:T(8,128)} %diff_hbm.1, f32[6,6]{1,0:T(8,128)} %mix_hbm.1, s32[16,128]{1,0:T(8,128)} %mask_hbm.1, bf16[54,128]{1,0:T(8,128)(2,1)} %bitcast.4, ...), custom_call_target="tpu_custom_call" | custom-call | tf_op jit(solution)/shard_map/ocean/pallas_call | solution.py:625
  35.6 0.7 %emit.1 = (f32[6,16,128]{2,1,0:T(8,128)}, f32[6,16,128]{2,1,0:T(8,128)}, f32[188,128]{1,0:T(8,128)}, f32[1]{0:T(128)}) custom-call(f32[6,16,128]{2,1,0:T(8,128)S(1)} %get-tuple-element.12.final_in, f32[6,16,128]{2,1,0:T(8,128)S(1)} %get-tuple-element.13.adjoint_in, f32[188,128]{1,0:T(8,128)S(1)} %get-tuple-element.14.params_in, ...), custom_call_target="tpu_custom_call" | custom-call | tf_op jit(solution)/shard_map/emit/pallas_call | solution.py:656

commit v5 on v4

--- a/solution.py
+++ b/solution.py
@@ -102,6 +102,7 @@
     send_south,
     edge,
     halo_in,
+    here_sem,
     send_sem,
     recv_sem,
     flat_a,
@@ -127,7 +128,10 @@
     weights_three,
     base_params,
     grads,
+    others_ref,
+    others,
     recv_one,
+    recv_others,
     recv_two,
     gathered,
     total_ref,
@@ -138,10 +142,8 @@
     west, east = ring(lon, -1, NLON), ring(lon, 1, NLON)
 
     barrier = pltpu.get_barrier_semaphore()
-    corners = [{"lat": a, "lon": b} for a in (north, south) for b in (west, east)]
-    greet = [{"lon": ring(lon, d, NLON)} for d in LON_STEPS[:5]] + corners
-    greet += [{"lat": ring(lat, d, NLAT)} for d in LAT_STEPS]
-    greet += [{"lon": ring(lon, d, NLON)} for d in LON_STEPS[5:]]
+    greet = [{"lat": a, "lon": b} for a in (north, south) for b in (west, east)]
+    greet += [{"lat": north}, {"lat": south}, {"lon": west}, {"lon": east}]
     for device in greet:
         pl.semaphore_signal(barrier, inc=1, device_id=device, device_id_type=MESH)
 
@@ -226,10 +228,21 @@
     for copy in halos:
         copy.start()
 
+    def tell(stage, reach):
+        devices = [{"lon": ring(lon, d, NLON)} for d in (reach, -reach)]
+        if reach < NLAT // 2:
+            devices += [{"lat": ring(lat, d, NLAT)} for d in (reach, -reach)]
+        for device in devices:
+            pl.semaphore_signal(here_sem.at[stage], inc=1, device_id=device, device_id_type=MESH)
+        return len(devices)
+
+    told = tell(0, 1)
+
     for load in loads[4:8]:
         load.wait()
     weights_one[...] = jnp.zeros_like(weights_one)
     weights_one[0:PATCH, :] = first_ref[...].astype(F32)
+    others_ref[...] = jnp.zeros_like(others_ref)
     weights_three[...] = jnp.zeros_like(weights_three)
     weights_three[0:FIELDS, :] = output_ref[...].astype(F32)
 
@@ -237,6 +250,9 @@
         return lax.dot_general(
             left, right, (((1,), (1,)), ((), ())), preferred_element_type=F32, precision=precision
         )
+
+    def tn(left, right):
+        return lax.dot_general(left, right, (((0,), (0,)), ((), ())), preferred_element_type=F32)
 
     deep_i = lax.broadcasted_iota(jnp.int32, (DEEP, HID), 0)
     deep_j = lax.broadcasted_iota(jnp.int32, (DEEP, HID), 1)
@@ -308,6 +324,9 @@
         mix_to.append(to_tile)
         mix_from.append(from_tile)
 
+    pl.semaphore_wait(here_sem.at[0], told)
+    told = tell(1, 2)
+
     def mixed(tiles, value):
         length = value.shape[1]
         total = None
@@ -316,6 +335,8 @@
             total = term if total is None else total + term
         return total
 
+    pl.semaphore_wait(here_sem.at[1], told)
+    told = tell(2, 4)
     all_halos = halo_copy(halo_in, halo_in, {"lon": east})
     all_halos.wait_recv()
 
@@ -431,9 +452,9 @@
                     block = block + spread
                 patch_grad[8 * k : 8 * k + 8, here] = block
         own = own_ref[:, grad_here]
-        grad_first = nt(back_one[:, grad_here], patch_ref[:, grad_here] * own[0:DEEP])
         grad_second = nt(back_two[:, grad_here], one_ref[:, grad_here] * own)
         grad_output = nt(out_grad[:, grad_here] * own[0:16], two_ref[:, grad_here])
+        grad_first = nt(patch_ref[:, grad_here] * own[0:DEEP], back_one[:, grad_here])
         return grad_first, grad_second, grad_output
 
     def scatter():
@@ -454,15 +475,6 @@
     first = first + late_first
     second = second + late_second
     output = output + late_output
-
-    high_part, low_part = halves(first)
-    narrow = jnp.dot(high_part, select, preferred_element_type=F32) + jnp.dot(
-        low_part, select, preferred_element_type=F32
-    )
-    others = jnp.concatenate([flatten_rows(narrow, True), output[0:8]], axis=0)
-    for i in range(NLON):
-        grads[i, 0:8, :] = second[8 * i : 8 * i + 8]
-        grads[i, 8:12, :] = others[4 * i : 4 * i + 4]
 
     def copies_along(axis, here, steps, size, phase, source, target):
         made = []
@@ -491,7 +503,16 @@
             device_id_type=MESH,
         )
 
+    for i in range(NLON):
+        grads[i] = second[8 * i : 8 * i + 8]
+    pl.semaphore_wait(here_sem.at[2], told)
     copies_along("lon", lon, LON_STEPS, NLON, 1, lambda peer: grads.at[peer], lambda place: recv_one.at[place])
+    for k in range(9):
+        others_ref[6 * k : 6 * k + 6, :] = first[8 * k : 8 * k + 6]
+    others_ref[56:64, :] = output[0:8]
+    for i in range(NLON):
+        others[i] = others_ref[4 * i : 4 * i + 4, :]
+    copies_along("lon", lon, LON_STEPS, NLON, 4, lambda peer: others.at[peer], lambda place: recv_others.at[place])
 
     write_rows(state_two, final_ref)
     adj_one[...] = scatter()
@@ -502,7 +523,13 @@
     band = grads[lon]
     for n in range(NLON - 1):
         band = band + recv_one[n]
-    recv_two[lat] = band
+    recv_two[lat, 0:8, :] = band
+    other_scatters = all_of(4, recv_others)
+    other_scatters.wait_recv()
+    band = others[lon]
+    for n in range(NLON - 1):
+        band = band + recv_others[n]
+    recv_two[lat, 8:CHUNK, :] = band
 
     copies_along("lat", lat, LAT_STEPS, NLAT, 2, lambda peer: recv_two.at[lat], lambda place: recv_two.at[lat])
     exchanges = all_of(2, recv_two.at[0 : NLAT - 1])
@@ -528,21 +555,23 @@
         square_sum = square_sum + value * value
         band_sum = band_sum + gathered[i, CHUNK : CHUNK + 1, :]
         total_ref[54 + 8 * i : 62 + 8 * i, :] = value[0:8]
-        if i < 13:
-            total_ref[4 * i : 4 * i + 4, :] = value[8:12]
-        elif i == 13:
-            total_ref[52:54, :] = value[8:10]
+        if i < 14:
+            others_ref[4 * i : 4 * i + 4, :] = value[8:12]
         elif i == 14:
             total_ref[182:186, :] = value[8:12]
         else:
             total_ref[186:188, :] = value[8:10]
+    others_ref[56:64, :] = jnp.zeros((8, LANES), F32)
+    high_part, low_part = halves(others_ref[...])
+    turned_total = tn(high_part, eye[0:64]) + tn(low_part, eye[0:64])
+    total_ref[0:PATCH, :] = flatten_rows(turned_total, True)[0:PATCH]
     grad_square = jnp.sum(square_sum)
     ratio_ref[...] = jnp.full((1, LANES), jnp.sum(band_sum) / (grad_square + epsilon), F32)
     spread_square = jnp.full((1, LANES), grad_square / PARAMS + epsilon, F32)
     scale = learn_rate / jnp.sqrt(spread_square)
     params_ref[...] = base_params[0:188, :] - scale * total_ref[0:188, :] + noise_in[...]
 
-    for copies in (all_halos, scatters, exchanges, collects):
+    for copies in (all_halos, scatters, other_scatters, exchanges, collects):
         copies.wait_send()
 
 
@@ -590,8 +619,9 @@
         vmem((6, 8, LANES), F32),
         vmem((2, 8, LANES), F32),
         vmem((24, 8, LANES), F32),
-        dma((4,)),
-        dma((4,)),
+        pltpu.SemaphoreType.REGULAR((3,)),
+        dma((5,)),
+        dma((5,)),
         flat8,
         flat8,
         hidden,
@@ -614,8 +644,11 @@
         vmem((HID, LANES), F32),
         vmem((16, LANES), F32),
         vmem((192, LANES), F32),
-        vmem((NLON, CHUNK, LANES), F32),
-        vmem((NLON - 1, CHUNK, LANES), F32),
+        vmem((NLON, 8, LANES), F32),
+        vmem((64, LANES), F32),
+        vmem((NLON, 4, LANES), F32),
+        vmem((NLON - 1, 8, LANES), F32),
+        vmem((NLON - 1, 4, LANES), F32),
         vmem((NLAT, CHUNK, LANES), F32),
         vmem((NLON, SENT, LANES), F32),
         vmem((192, LANES), F32),

time: 36.4 us -> 37 us (1.016)
  Pallas kernels: 35.6 us -> 36.2 us
    pallas_call x1, Pallas kernels: 34.9 us -> 35.5 us  [on_device(): pl.pallas_call(kernel, out_shape=(jax.ShapeDtypeStruct((FIELDS, ROWS, COL...]
where the time goes in v5:
time: 37 us; the launch traced here: 36.8 us
  Pallas kernels  36.2 us (98%)
  between operations  0.64 us (2%)
    pallas_call x1, Pallas kernels, on_device(): pl.pallas_call(kernel, out_shape=(jax.ShapeDtypeStruct((FIELDS, ROWS, COL...  35.5 us

profile of v5, /device:TPU:1, one launch (start us, length us, event | category | flops | bytes accessed | tf_op | source)
XLA Modules:
  0.0 36.8 jit_solution(14121633873317863383)
XLA Ops:
  0.6 35.5 %ocean.1 = (f32[6,16,128]{2,1,0:T(8,128)S(1)}, f32[6,16,128]{2,1,0:T(8,128)S(1)}, f32[188,128]{1,0:T(8,128)S(1)}, f32[1,128]{1,0:T(1,128)S(1)}) custom-call(f32[6,16,128]{2,1,0:T(8,128)} %state_hbm.1, f32[16,128]{1,0:T(8,128)} %diff_hbm.1, f32[6,6]{1,0:T(8,128)} %mix_hbm.1, s32[16,128]{1,0:T(8,128)} %mask_hbm.1, bf16[54,128]{1,0:T(8,128)(2,1)} %bitcast.4, ...), custom_call_target="tpu_custom_call" | custom-call | tf_op jit(solution)/shard_map/ocean/pallas_call | solution.py:658
  36.1 0.7 %emit.1 = (f32[6,16,128]{2,1,0:T(8,128)}, f32[6,16,128]{2,1,0:T(8,128)}, f32[188,128]{1,0:T(8,128)}, f32[1]{0:T(128)}) custom-call(f32[6,16,128]{2,1,0:T(8,128)S(1)} %get-tuple-element.12.final_in, f32[6,16,128]{2,1,0:T(8,128)S(1)} %get-tuple-element.13.adjoint_in, f32[188,128]{1,0:T(8,128)S(1)} %get-tuple-element.14.params_in, ...), custom_call_target="tpu_custom_call" | custom-call | tf_op jit(solution)/shard_map/emit/pallas_call | solution.py:689

commit v6 on v5

--- a/solution.py
+++ b/solution.py
@@ -30,9 +30,12 @@
 DEEP = 80
 PARAMS = 24064
 NLON, NLAT = 16, 8
-CHUNK = 12
+CHUNKS = 8
+CHUNK = 24
 SENT = CHUNK + 1
-LON_STEPS = (8, 7, 9, 6, 10, 5, 11, 4, 12, 3, 13, 2, 14, 1, 15)
+CHIP_STEPS = (8, 6, 10, 4, 12, 2, 14)
+NEAR_STEPS = (4, 13, 3, 14, 2, 15, 1)
+LON_STEPS = (8, 6, 10, 4, 12, 3, 13, 2, 14, 1, 15)
 LAT_STEPS = (2, 6, 1, 3, 5, 7, 4)
 
 
@@ -127,11 +130,12 @@
     weights_one,
     weights_three,
     base_params,
+    seconds,
+    others,
+    twin_seconds,
+    twin_others,
     grads,
-    others_ref,
-    others,
     recv_one,
-    recv_others,
     recv_two,
     gathered,
     total_ref,
@@ -242,7 +246,6 @@
         load.wait()
     weights_one[...] = jnp.zeros_like(weights_one)
     weights_one[0:PATCH, :] = first_ref[...].astype(F32)
-    others_ref[...] = jnp.zeros_like(others_ref)
     weights_three[...] = jnp.zeros_like(weights_three)
     weights_three[0:FIELDS, :] = output_ref[...].astype(F32)
 
@@ -250,9 +253,6 @@
         return lax.dot_general(
             left, right, (((1,), (1,)), ((), ())), preferred_element_type=F32, precision=precision
         )
-
-    def tn(left, right):
-        return lax.dot_general(left, right, (((0,), (0,)), ((), ())), preferred_element_type=F32)
 
     deep_i = lax.broadcasted_iota(jnp.int32, (DEEP, HID), 0)
     deep_j = lax.broadcasted_iota(jnp.int32, (DEEP, HID), 1)
@@ -454,7 +454,7 @@
         own = own_ref[:, grad_here]
         grad_second = nt(back_two[:, grad_here], one_ref[:, grad_here] * own)
         grad_output = nt(out_grad[:, grad_here] * own[0:16], two_ref[:, grad_here])
-        grad_first = nt(patch_ref[:, grad_here] * own[0:DEEP], back_one[:, grad_here])
+        grad_first = nt(back_one[:, grad_here], patch_ref[:, grad_here] * own[0:DEEP])
         return grad_first, grad_second, grad_output
 
     def scatter():
@@ -503,33 +503,56 @@
             device_id_type=MESH,
         )
 
-    for i in range(NLON):
-        grads[i] = second[8 * i : 8 * i + 8]
+    core = lax.rem(lon, 2)
+    chip = lax.div(lon, 2)
+    twin = lon + 1 - 2 * core
+
+    def twin_copy(phase, source, target):
+        return pltpu.make_async_remote_copy(
+            src_ref=source.at[1 - core],
+            dst_ref=target,
+            send_sem=send_sem.at[phase],
+            recv_sem=recv_sem.at[phase],
+            device_id={"lon": twin},
+            device_id_type=MESH,
+        )
+
+    for c in range(CHUNKS):
+        seconds[c % 2, c // 2] = second[16 * c : 16 * c + 16]
+    twin_second = twin_copy(4, seconds, twin_seconds)
+    twin_second.start()
+    high_part, low_part = halves(first)
+    narrow = jnp.dot(high_part, select, preferred_element_type=F32) + jnp.dot(
+        low_part, select, preferred_element_type=F32
+    )
+    flat_first = flatten_rows(narrow, True)
+    for c in range(CHUNKS):
+        others[c % 2, c // 2] = flat_first[8 * c : 8 * c + 8] if c < CHUNKS - 1 else output[0:8]
+    twin_other = twin_copy(5, others, twin_others)
+    twin_other.start()
+    twin_second.wait_recv()
+    for m in range(CHUNKS // 2):
+        grads[m, 0:16, :] = seconds[core, m] + twin_seconds[m]
+    twin_other.wait_recv()
+    for m in range(CHUNKS // 2):
+        grads[m, 16:CHUNK, :] = others[core, m] + twin_others[m]
     pl.semaphore_wait(here_sem.at[2], told)
-    copies_along("lon", lon, LON_STEPS, NLON, 1, lambda peer: grads.at[peer], lambda place: recv_one.at[place])
-    for k in range(9):
-        others_ref[6 * k : 6 * k + 6, :] = first[8 * k : 8 * k + 6]
-    others_ref[56:64, :] = output[0:8]
-    for i in range(NLON):
-        others[i] = others_ref[4 * i : 4 * i + 4, :]
-    copies_along("lon", lon, LON_STEPS, NLON, 4, lambda peer: others.at[peer], lambda place: recv_others.at[place])
+    copies_along(
+        "lon", lon, CHIP_STEPS, NLON, 1,
+        lambda peer: grads.at[lax.rem(lax.div(peer, 2), 4)], lambda place: recv_one.at[chip],
+    )
+    recv_one[chip] = grads[lax.rem(chip, 4)]
 
     write_rows(state_two, final_ref)
     adj_one[...] = scatter()
     write_rows(adj_one, adjoint_ref)
 
-    scatters = all_of(1, recv_one)
+    scatters = all_of(1, recv_one.at[0 : NLON // 2 - 1])
     scatters.wait_recv()
-    band = grads[lon]
-    for n in range(NLON - 1):
+    band = recv_one[0]
+    for n in range(1, NLON // 2):
         band = band + recv_one[n]
-    recv_two[lat, 0:8, :] = band
-    other_scatters = all_of(4, recv_others)
-    other_scatters.wait_recv()
-    band = others[lon]
-    for n in range(NLON - 1):
-        band = band + recv_others[n]
-    recv_two[lat, 8:CHUNK, :] = band
+    recv_two[lat] = band
 
     copies_along("lat", lat, LAT_STEPS, NLAT, 2, lambda peer: recv_two.at[lat], lambda place: recv_two.at[lat])
     exchanges = all_of(2, recv_two.at[0 : NLAT - 1])
@@ -540,38 +563,35 @@
         value = recv_two[b]
         total = total + value
         squares = squares + value * value
-    gathered[lon, 0:CHUNK, :] = total
-    gathered[lon, CHUNK:SENT, :] = jnp.sum(squares, axis=0, keepdims=True)
-
-    copies_along("lon", lon, LON_STEPS, NLON, 3, lambda peer: gathered.at[lon], lambda place: gathered.at[lon])
+    mine = lax.rem(lon, CHUNKS)
+    gathered[mine, 0:CHUNK, :] = total
+    gathered[mine, CHUNK:SENT, :] = jnp.sum(squares, axis=0, keepdims=True)
+
+    copies_along("lon", lon, NEAR_STEPS, NLON, 3, lambda peer: gathered.at[mine], lambda place: gathered.at[mine])
     loads[8].wait()
-    collects = all_of(3, gathered.at[0 : NLON - 1])
+    collects = all_of(3, gathered.at[0 : CHUNKS - 1])
     collects.wait_recv()
 
     square_sum = jnp.zeros((CHUNK, LANES), F32)
     band_sum = jnp.zeros((1, LANES), F32)
-    for i in range(NLON):
-        value = gathered[i, 0:CHUNK, :]
+    for c in range(CHUNKS):
+        value = gathered[c, 0:CHUNK, :]
         square_sum = square_sum + value * value
-        band_sum = band_sum + gathered[i, CHUNK : CHUNK + 1, :]
-        total_ref[54 + 8 * i : 62 + 8 * i, :] = value[0:8]
-        if i < 14:
-            others_ref[4 * i : 4 * i + 4, :] = value[8:12]
-        elif i == 14:
-            total_ref[182:186, :] = value[8:12]
+        band_sum = band_sum + gathered[c, CHUNK:SENT, :]
+        total_ref[54 + 16 * c : 70 + 16 * c, :] = value[0:16]
+        if c < 6:
+            total_ref[8 * c : 8 * c + 8, :] = value[16:24]
+        elif c == 6:
+            total_ref[48:54, :] = value[16:22]
         else:
-            total_ref[186:188, :] = value[8:10]
-    others_ref[56:64, :] = jnp.zeros((8, LANES), F32)
-    high_part, low_part = halves(others_ref[...])
-    turned_total = tn(high_part, eye[0:64]) + tn(low_part, eye[0:64])
-    total_ref[0:PATCH, :] = flatten_rows(turned_total, True)[0:PATCH]
-    grad_square = jnp.sum(square_sum)
-    ratio_ref[...] = jnp.full((1, LANES), jnp.sum(band_sum) / (grad_square + epsilon), F32)
-    spread_square = jnp.full((1, LANES), grad_square / PARAMS + epsilon, F32)
-    scale = learn_rate / jnp.sqrt(spread_square)
+            total_ref[182:188, :] = value[16:22]
+    grad_square = jnp.sum(jnp.sum(square_sum, axis=0, keepdims=True), axis=1, keepdims=True)
+    band_square = jnp.sum(band_sum, axis=1, keepdims=True)
+    ratio_ref[...] = jnp.broadcast_to(band_square / (grad_square + epsilon), (1, LANES))
+    scale = learn_rate / jnp.sqrt(jnp.broadcast_to(grad_square, (1, LANES)) / PARAMS + epsilon)
     params_ref[...] = base_params[0:188, :] - scale * total_ref[0:188, :] + noise_in[...]
 
-    for copies in (all_halos, scatters, other_scatters, exchanges, collects):
+    for copies in (all_halos, twin_second, twin_other, scatters, exchanges, collects):
         copies.wait_send()
 
 
@@ -620,8 +640,8 @@
         vmem((2, 8, LANES), F32),
         vmem((24, 8, LANES), F32),
         pltpu.SemaphoreType.REGULAR((3,)),
-        dma((5,)),
-        dma((5,)),
+        dma((6,)),
+        dma((6,)),
         flat8,
         flat8,
         hidden,
@@ -644,13 +664,14 @@
         vmem((HID, LANES), F32),
         vmem((16, LANES), F32),
         vmem((192, LANES), F32),
-        vmem((NLON, 8, LANES), F32),
-        vmem((64, LANES), F32),
-        vmem((NLON, 4, LANES), F32),
-        vmem((NLON - 1, 8, LANES), F32),
-        vmem((NLON - 1, 4, LANES), F32),
+        vmem((2, CHUNKS // 2, 16, LANES), F32),
+        vmem((2, CHUNKS // 2, 8, LANES), F32),
+        vmem((CHUNKS // 2, 16, LANES), F32),
+        vmem((CHUNKS // 2, 8, LANES), F32),
+        vmem((CHUNKS // 2, CHUNK, LANES), F32),
+        vmem((NLON // 2, CHUNK, LANES), F32),
         vmem((NLAT, CHUNK, LANES), F32),
-        vmem((NLON, SENT, LANES), F32),
+        vmem((CHUNKS, SENT, LANES), F32),
         vmem((192, LANES), F32),
     ]
     hbm = pl.BlockSpec(memory_space=pltpu.HBM)

time: 37 us -> 36.1 us (0.976)
  Pallas kernels: 36.2 us -> 35.3 us
    pallas_call x1, Pallas kernels: 35.5 us -> 34.6 us  [on_device(): pl.pallas_call(kernel, out_shape=(jax.ShapeDtypeStruct((FIELDS, ROWS, COL...]
where the time goes in v6:
time: 36.1 us; the launch traced here: 35.9 us
  Pallas kernels  35.3 us (98%)
  between operations  0.64 us (2%)
    pallas_call x1, Pallas kernels, on_device(): pl.pallas_call(kernel, out_shape=(jax.ShapeDtypeStruct((FIELDS, ROWS, COL...  34.6 us

profile of v6, /device:TPU:1, one launch (start us, length us, event | category | flops | bytes accessed | tf_op | source)
XLA Modules:
  0.0 35.9 jit_solution(14382912586294185171)
XLA Ops:
  0.6 34.6 %ocean.1 = (f32[6,16,128]{2,1,0:T(8,128)S(1)}, f32[6,16,128]{2,1,0:T(8,128)S(1)}, f32[188,128]{1,0:T(8,128)S(1)}, f32[1,128]{1,0:T(1,128)S(1)}) custom-call(f32[6,16,128]{2,1,0:T(8,128)} %state_hbm.1, f32[16,128]{1,0:T(8,128)} %diff_hbm.1, f32[6,6]{1,0:T(8,128)} %mix_hbm.1, s32[16,128]{1,0:T(8,128)} %mask_hbm.1, bf16[54,128]{1,0:T(8,128)(2,1)} %bitcast.4, ...), custom_call_target="tpu_custom_call" | custom-call | tf_op jit(solution)/shard_map/ocean/pallas_call | solution.py:679
  35.2 0.7 %emit.1 = (f32[6,16,128]{2,1,0:T(8,128)}, f32[6,16,128]{2,1,0:T(8,128)}, f32[188,128]{1,0:T(8,128)}, f32[1]{0:T(128)}) custom-call(f32[6,16,128]{2,1,0:T(8,128)S(1)} %get-tuple-element.12.final_in, f32[6,16,128]{2,1,0:T(8,128)S(1)} %get-tuple-element.13.adjoint_in, f32[188,128]{1,0:T(8,128)S(1)} %get-tuple-element.14.params_in, ...), custom_call_target="tpu_custom_call" | custom-call | tf_op jit(solution)/shard_map/emit/pallas_call | solution.py:710

commit v7 on v6

--- a/solution.py
+++ b/solution.py
@@ -247,6 +247,8 @@
     weights_one[...] = jnp.zeros_like(weights_one)
     weights_one[0:PATCH, :] = first_ref[...].astype(F32)
     weights_three[...] = jnp.zeros_like(weights_three)
+    state_one[...] = jnp.zeros_like(state_one)
+    patch_grad[...] = jnp.zeros_like(patch_grad)
     weights_three[0:FIELDS, :] = output_ref[...].astype(F32)
 
     def nt(left, right, precision=None):
@@ -405,7 +407,6 @@
             )
             next_ref[:, here] = wide_mask[:, here] * update
 
-    state_one[...] = jnp.zeros_like(state_one)
     make_patch(flat_a[...], patch_zero)
     low, high = tile_range(3)
     forward(flat_a, patch_zero, hid_one_zero, hid_two_zero, state_one, low, high, low, high)
@@ -466,7 +467,6 @@
             total = block if total is None else total + block
         return total
 
-    patch_grad[...] = jnp.zeros_like(patch_grad)
     low, high = tile_range(2)
     late_first, late_second, late_output = backward(flat_b, patch_one, hid_one_one, hid_two_one, low, high)
     adj_one[...] = scatter()

time: 36.1 us -> 36.1 us (level)
  no operation moved by 1% of the time
where the time goes in v7:
time: 36.1 us; the launch traced here: 35.9 us
  Pallas kernels  35.3 us (98%)
  between operations  0.64 us (2%)
    pallas_call x1, Pallas kernels, on_device(): pl.pallas_call(kernel, out_shape=(jax.ShapeDtypeStruct((FIELDS, ROWS, COL...  34.6 us

profile of v7, /device:TPU:1, one launch (start us, length us, event | category | flops | bytes accessed | tf_op | source)
XLA Modules:
  0.0 35.9 jit_solution(14382912586294185171)
XLA Ops:
  0.6 34.6 %ocean.1 = (f32[6,16,128]{2,1,0:T(8,128)S(1)}, f32[6,16,128]{2,1,0:T(8,128)S(1)}, f32[188,128]{1,0:T(8,128)S(1)}, f32[1,128]{1,0:T(1,128)S(1)}) custom-call(f32[6,16,128]{2,1,0:T(8,128)} %state_hbm.1, f32[16,128]{1,0:T(8,128)} %diff_hbm.1, f32[6,6]{1,0:T(8,128)} %mix_hbm.1, s32[16,128]{1,0:T(8,128)} %mask_hbm.1, bf16[54,128]{1,0:T(8,128)(2,1)} %bitcast.4, ...), custom_call_target="tpu_custom_call" | custom-call | tf_op jit(solution)/shard_map/ocean/pallas_call | solution.py:679
  35.2 0.7 %emit.1 = (f32[6,16,128]{2,1,0:T(8,128)}, f32[6,16,128]{2,1,0:T(8,128)}, f32[188,128]{1,0:T(8,128)}, f32[1]{0:T(128)}) custom-call(f32[6,16,128]{2,1,0:T(8,128)S(1)} %get-tuple-element.12.final_in, f32[6,16,128]{2,1,0:T(8,128)S(1)} %get-tuple-element.13.adjoint_in, f32[188,128]{1,0:T(8,128)S(1)} %get-tuple-element.14.params_in, ...), custom_call_target="tpu_custom_call" | custom-call | tf_op jit(solution)/shard_map/emit/pallas_call | solution.py:710

commit v8 on v7

--- a/solution.py
+++ b/solution.py
@@ -125,6 +125,9 @@
     back_one,
     back_two,
     out_grad,
+    late_one,
+    late_two,
+    late_out,
     patch_grad,
     adj_one,
     weights_one,
@@ -426,7 +429,7 @@
     grad_low, grad_high = tile_range(0)
     grad_here = slice(grad_low, grad_high)
 
-    def backward(adj_ref, patch_ref, one_ref, two_ref, low, high):
+    def backward(adj_ref, patch_ref, one_ref, two_ref, back_one, back_two, out_grad, low, high):
         for start, size in chunks(low, high):
             here = slice(start, start + size)
             masked = wide_mask[:, here] * adj_ref[:, here]
@@ -452,6 +455,8 @@
                 elif k % 2:
                     block = block + spread
                 patch_grad[8 * k : 8 * k + 8, here] = block
+
+    def gradients(patch_ref, one_ref, two_ref, back_one, back_two, out_grad):
         own = own_ref[:, grad_here]
         grad_second = nt(back_two[:, grad_here], one_ref[:, grad_here] * own)
         grad_output = nt(out_grad[:, grad_here] * own[0:16], two_ref[:, grad_here])
@@ -468,10 +473,16 @@
         return total
 
     low, high = tile_range(2)
-    late_first, late_second, late_output = backward(flat_b, patch_one, hid_one_one, hid_two_one, low, high)
+    backward(
+        flat_b, patch_one, hid_one_one, hid_two_one, late_one, late_two, late_out, low, high
+    )
     adj_one[...] = scatter()
+    late_first, late_second, late_output = gradients(patch_one, hid_one_one, hid_two_one, late_one, late_two, late_out)
     low, high = tile_range(1)
-    first, second, output = backward(adj_one, patch_zero, hid_one_zero, hid_two_zero, low, high)
+    backward(
+        adj_one, patch_zero, hid_one_zero, hid_two_zero, back_one, back_two, out_grad, low, high
+    )
+    first, second, output = gradients(patch_zero, hid_one_zero, hid_two_zero, back_one, back_two, out_grad)
     first = first + late_first
     second = second + late_second
     output = output + late_output
@@ -656,6 +667,9 @@
         hidden,
         hidden,
         hidden,
+        hidden,
+        hidden,
+        vmem((16, FLAT), BF16),
         hidden,
         hidden,
         vmem((16, FLAT), BF16),

time: 36.1 us -> 36 us (level)
  no operation moved by 1% of the time
where the time goes in v8:
time: 36 us; the launch traced here: 35.9 us
  Pallas kernels  35.2 us (98%)
  between operations  0.64 us (2%)
    pallas_call x1, Pallas kernels, on_device(): pl.pallas_call(kernel, out_shape=(jax.ShapeDtypeStruct((FIELDS, ROWS, COL...  34.5 us

profile of v8, /device:TPU:1, one launch (start us, length us, event | category | flops | bytes accessed | tf_op | source)
XLA Modules:
  0.0 35.9 jit_solution(2168242166489533933)
XLA Ops:
  0.6 34.5 %ocean.1 = (f32[6,16,128]{2,1,0:T(8,128)S(1)}, f32[6,16,128]{2,1,0:T(8,128)S(1)}, f32[188,128]{1,0:T(8,128)S(1)}, f32[1,128]{1,0:T(1,128)S(1)}) custom-call(f32[6,16,128]{2,1,0:T(8,128)} %state_hbm.1, f32[16,128]{1,0:T(8,128)} %diff_hbm.1, f32[6,6]{1,0:T(8,128)} %mix_hbm.1, s32[16,128]{1,0:T(8,128)} %mask_hbm.1, bf16[54,128]{1,0:T(8,128)(2,1)} %bitcast.4, ...), custom_call_target="tpu_custom_call" | custom-call | tf_op jit(solution)/shard_map/ocean/pallas_call | solution.py:693
  35.1 0.7 %emit.1 = (f32[6,16,128]{2,1,0:T(8,128)}, f32[6,16,128]{2,1,0:T(8,128)}, f32[188,128]{1,0:T(8,128)}, f32[1]{0:T(128)}) custom-call(f32[6,16,128]{2,1,0:T(8,128)S(1)} %get-tuple-element.12.final_in, f32[6,16,128]{2,1,0:T(8,128)S(1)} %get-tuple-element.13.adjoint_in, f32[188,128]{1,0:T(8,128)S(1)} %get-tuple-element.14.params_in, ...), custom_call_target="tpu_custom_call" | custom-call | tf_op jit(solution)/shard_map/emit/pallas_call | solution.py:724
